TPU v7x, 512 devices: a whole 4x4x16 slice. The times are simulated.
512 devices in a mesh: sp: 32 (over z, x_hi), tp: 16 (over x_lo, y, core).
Axes of the slice: x: 4 (x_hi: 2, x_lo: 2; x = x_hi * 2 + x_lo), y: 4, z: 16, core: 2. Of those that a mesh axis runs over, the one named last changes fastest.
Arguments:
- tokens: bfloat16 [2, 128, 32, 3072], P(None, 'sp', None, 'tp'), may hold values from -6 to 6
- qkv_weight: bfloat16 [2, 3072, 3, 2048], P(None, 'sp', None, 'tp'), may hold values from -0.109375 to 0.109375
- out_weight: bfloat16 [2, 2048, 3072], P(None, 'tp', 'sp'), may hold values from -0.125 to 0.125
- norm_gain: float32 [2, 3072], replicated, may hold values from 0.5 to 1.5
- qk_gain: float32 [2, 2, 128], replicated, may hold values from 0.25 to 1.75
- shifts: int32 [2, 2], replicated, may hold values from 0 to 7, as said below
Outputs:
- restored: bfloat16 [2, 128, 32, 3072], P(None, 'sp', None, 'tp')
Inputs may be any that keep to these rules, and one draw needn't show every extreme that they name: shifts[1] equals shifts[0] plus 4//2 along rows and 4 along columns, modulo 4 and 8; every column offset is 3 or 7.
All inputs are finite; a program needn't handle non-finite values.
Results may differ from a plain program's by a relative error of at most 0.015.
Values may be sent and summed in bfloat16 or wider, within the bound.
No kernel may reach another device: no remote copies, remote signals or barrier semaphores. Data moves between devices by JAX's collectives and lax.ppermute only.
A program may use at most 64 MiB of HBM per device.

v0:
```python
import math

import jax
import jax.numpy as jnp
from jax import lax
from jax.sharding import PartitionSpec as P

WH = 4
WW = 8


def with_halo(block, sides, width):
    for axis, dim in sides:
        count = lax.axis_size(axis)
        forward = [(i, i + 1) for i in range(count - 1)]
        backward = [(target, source) for source, target in forward]
        low = lax.ppermute(
            lax.slice_in_dim(block, block.shape[dim] - width, None, axis=dim), axis, forward
        )
        high = lax.ppermute(lax.slice_in_dim(block, 0, width, axis=dim), axis, backward)
        block = jnp.concatenate([low, block, high], axis=dim)
    return block


def normalize(inputs, scale_gain):
    mean_square = jnp.mean(inputs * inputs, axis=-1, keepdims=True)
    return inputs * lax.rsqrt(mean_square + 1e-06) * scale_gain


def window_mask(
    first_row, slab_rows, band_rows, slab_cols, frames, total_rows, shift_row, shift_col
):
    query_row = first_row + jnp.arange(slab_rows, dtype=jnp.int32)
    key_row = first_row - WH + jnp.arange(band_rows, dtype=jnp.int32)
    column = jnp.arange(slab_cols, dtype=jnp.int32)
    query_win = (query_row + shift_row) // WH
    key_win = (key_row + shift_row) // WH
    column_win = (column + shift_col) // WW
    valid = (key_row >= 0) & (key_row < total_rows)
    same_row = (query_win[:, None] == key_win[None, :]) & valid[None, :]
    same_col = column_win[:, None] == column_win[None, :]
    small = same_row[:, None, :, None] & same_col[None, :, None, :]
    small = small.reshape(slab_rows * slab_cols, band_rows * slab_cols)
    whole = jnp.broadcast_to(
        small[None, :, None, :], (frames, slab_rows * slab_cols, frames, band_rows * slab_cols)
    )
    return whole.reshape(frames * slab_rows * slab_cols, frames * band_rows * slab_cols).astype(
        jnp.float32
    )


def on_device(tokens, qkv_weight, out_weight, norm_gain, qk_gain, shifts):
    frames, slab_rows, slab_cols, local_width = tokens.shape
    token_count = frames * slab_rows * slab_cols
    local_rows = tokens.reshape(token_count, local_width)
    tp_rank = lax.axis_index("tp")
    first_row = lax.axis_index("sp") * slab_rows
    total_rows = slab_rows * lax.axis_size("sp")
    band_rows = slab_rows + 2 * WH

    def project_in(normed, which_block):
        local_weight = qkv_weight[which_block]
        local_weight = local_weight.reshape(local_weight.shape[0], -1)
        return jnp.dot(
            normed,
            lax.all_gather(local_weight, "sp", axis=0, tiled=True),
            preferred_element_type=jnp.float32,
        )

    def project_out(attended, which_block):
        return jnp.dot(
            attended,
            lax.all_gather(out_weight[which_block], "sp", axis=1, tiled=True),
            preferred_element_type=jnp.float32,
        )

    def attend_block(full_in, which_block):
        normed = normalize(full_in.astype(jnp.float32), norm_gain[which_block]).astype(jnp.bfloat16)
        projected = project_in(normed, which_block)
        head_width = qk_gain.shape[-1]
        heads_local = projected.shape[1] // (3 * head_width)
        projected = projected.reshape(token_count, 3, heads_local, head_width)
        queries = normalize(projected[:, 0], qk_gain[which_block, 0]).astype(jnp.bfloat16)
        key_rows = normalize(projected[:, 1], qk_gain[which_block, 1]).astype(jnp.bfloat16)
        value_rows = projected[:, 2].astype(jnp.bfloat16)
        key_value = jnp.stack([key_rows, value_rows]).reshape(
            2, frames, slab_rows, slab_cols, heads_local * head_width
        )
        widened = with_halo(key_value, (("sp", 2),), WH)
        band_keys = widened[0].reshape(frames * band_rows * slab_cols, heads_local, head_width)
        band_values = widened[1].reshape(frames * band_rows * slab_cols, heads_local, head_width)
        scores = jnp.einsum("qhd,khd->hqk", queries, band_keys, preferred_element_type=jnp.float32)
        scores = scores * (1.0 / math.sqrt(head_width))
        inside = window_mask(
            first_row,
            slab_rows,
            band_rows,
            slab_cols,
            frames,
            total_rows,
            shifts[which_block, 0],
            shifts[which_block, 1],
        )
        weights = jnp.exp(scores) * inside[None]
        normalized = (weights / jnp.sum(weights, axis=-1, keepdims=True)).astype(jnp.bfloat16)
        attended = jnp.einsum(
            "hqk,khd->qhd", normalized, band_values, preferred_element_type=jnp.float32
        )
        return attended.astype(jnp.bfloat16).reshape(token_count, heads_local * head_width)

    full_in = lax.all_gather(local_rows, "tp", axis=1, tiled=True)
    attended = attend_block(full_in, 0)
    partial_value = project_out(attended, 0)
    shares = lax.psum_scatter(
        partial_value.astype(jnp.bfloat16), "tp", scatter_dimension=1, tiled=True
    ).astype(jnp.float32)
    middle_local = (local_rows.astype(jnp.float32) + shares).astype(jnp.bfloat16)
    middle = lax.all_gather(middle_local, "tp", axis=1, tiled=True)
    attended = attend_block(middle, 1)
    partial_value = project_out(attended, 1)
    shares = lax.psum_scatter(
        partial_value.astype(jnp.bfloat16), "tp", scatter_dimension=1, tiled=True
    ).astype(jnp.float32)
    own_part = lax.dynamic_slice_in_dim(middle, tp_rank * local_width, local_width, 1)
    result = (own_part.astype(jnp.float32) + shares).astype(jnp.bfloat16)
    return result.reshape(frames, slab_rows, slab_cols, local_width)


def solution(mesh):
    placed = (
        P(None, "sp", None, "tp"),
        P(None, "sp", None, "tp"),
        P(None, "tp", "sp"),
        P(),
        P(),
        P(),
    )
    return jax.shard_map(
        on_device, mesh=mesh, in_specs=placed, out_specs=P(None, "sp", None, "tp"), check_vma=False
    )
```

profile of v0, /device:TPU:1, one launch (start us, length us, event | category | flops | bytes accessed | tf_op | source)
XLA Modules:
  0.0 589.0 jit_solution(17922230419037024840)
XLA Ops:
  6.5 1.6 copy.37
  8.2 0.0 all-gather.9.cloned.1.call-start
  8.3 0.9 fusion.36
  9.2 0.1 copy.39
  9.3 0.6 copy.61
  9.9 0.0 reduce-scatter.3.cloned.1.call-start
  10.0 1.4 fusion.39
  11.4 0.6 and_select_fusion.3
  12.1 1.2 and_select_fusion.1
  13.3 1.2 and_select_fusion.2
  14.4 0.8 slice_bitcast_fusion
  15.2 0.1 broadcast_compare_fusion.1
  15.3 0.1 compare_and_fusion
  15.4 0.8 fusion.37
  16.1 74.5 %all-gather = bf16[1,128,3072]{1,2,0:T(8,128)(2,1)S(1)} all-gather(bf16[1,128,96]{1,2,0:T(8,128)(2,1)S(1)} %get-tuple-element.18), channel_id=2, replica_groups=mesh['sp'=32,'tp'=16] {'sp'}, dimensions={2}, use_global_device_ids=true | all-gather | bytes 811008 | tf_op jit(solution)/shard_map/all_gather | solution.py:73
  90.6 0.8 fusion.38
  91.5 1.8 fusion
  93.3 109.8 %all-gather.9.cloned.1.call-done = bf16[3072,384]{1,0:T(8,128)(2,1)} async-done(((bf16[96,384]{1,0:T(8,128)(2,1)}), bf16[3072,384]{1,0:T(8,128)(2,1)}) %all-gather.9.cloned.1.call-update) | async-done | bytes 2359312 | tf_op jit(solution)/shard_map/all_gather | solution.py:66
  203.2 3.6 fusion.8
  206.8 0.1 rsqrt.56
  206.9 0.1 copy.41
  207.0 0.1 copy.42
  207.1 0.1 multiply_convert_fusion.3
  207.2 2.2 collective-permute-start
  209.4 1.3 collective-permute-start.1
  210.7 0.3 broadcast_and_fusion.1
  211.0 0.3 and.172
  211.3 0.2 copy.43
  211.4 0.2 broadcast_in_dim.4
  211.7 0.1 copy.55
  211.8 5.6 collective-permute-done.1
  217.5 0.5 fusion.40
  218.0 2.2 convolution_convert_fusion.1
  220.2 0.0 all-gather.11.cloned.1.call-start
  220.3 76.1 %reduce-scatter.3.cloned.1.call-done = bf16[256,192]{0,1:T(8,128)(2,1)} async-done(((bf16[256,3072]{0,1:T(8,128)(2,1)}), bf16[256,192]{0,1:T(8,128)(2,1)}) %reduce-scatter.3.cloned.1.call-update) | async-done | bytes 98320 | tf_op jit(solution)/shard_map/reduce_scatter | solution.py:114
  296.4 1.6 add_convert_fusion.1
  298.0 0.0 all-gather.13.cloned.1.call-start
  298.0 0.1 copy.45
  298.1 0.6 copy.60
  298.8 0.0 reduce-scatter.5.cloned.1.call-start
  298.8 0.6 and_select_fusion
  299.5 0.1 broadcast_compare_fusion
  299.5 0.3 broadcast_and_fusion
  299.8 0.3 and.180
  300.1 0.2 copy.49
  300.2 0.2 broadcast_in_dim.5
  300.5 0.1 copy.57
  300.6 66.5 %all-gather.1 = bf16[1,128,3072]{1,2,0:T(8,128)(2,1)S(1)} all-gather(bf16[1,128,96]{1,2,0:T(8,128)(2,1)S(1)} %get-tuple-element.17), channel_id=3, replica_groups=mesh['sp'=32,'tp'=16] {'sp'}, dimensions={2}, use_global_device_ids=true | all-gather | bytes 811008 | tf_op jit(solution)/shard_map/all_gather | solution.py:73
  367.1 1.8 fusion.3
  368.9 118.3 %all-gather.13.cloned.1.call-done = bf16[3072,384]{1,0:T(8,128)(2,1)} async-done(((bf16[96,384]{1,0:T(8,128)(2,1)}), bf16[3072,384]{1,0:T(8,128)(2,1)}) %all-gather.13.cloned.1.call-update) | async-done | bytes 2359312 | tf_op jit(solution)/shard_map/all_gather | solution.py:66
  487.2 3.6 fusion.6
  490.9 0.1 copy.47
  491.0 0.1 rsqrt.60
  491.1 0.1 copy.48
  491.2 0.1 multiply_convert_fusion.1
  491.3 2.2 collective-permute-start.2
  493.5 1.3 collective-permute-start.3
  494.8 0.6 collective-permute-done.2
  495.4 6.0 %collective-permute-done.3 = bf16[2,2,4,32,128]{4,3,2,1,0:T(8,128)(2,1)S(1)} collective-permute-done((bf16[2,2,4,32,128]{4,3,2,1,0:T(8,128)(2,1)S(1)}, bf16[2,2,4,32,128]{4,3,2,1,0:T(8,128)(2,1)S(1)}, u32[]{:S(2)}, u32[]{:S(2)}) %collective-permute-start.3) | collective-permute-done | bytes 131104 | tf_op jit(solution)/shard_map/ppermute | solution.py:20
  501.5 0.5 fusion.41
  502.0 2.2 convolution_convert_fusion
  504.3 76.1 %reduce-scatter.5.cloned.1.call-done = bf16[256,192]{0,1:T(8,128)(2,1)} async-done(((bf16[256,3072]{0,1:T(8,128)(2,1)}), bf16[256,192]{0,1:T(8,128)(2,1)}) %reduce-scatter.5.cloned.1.call-update) | async-done | bytes 98320 | tf_op jit(solution)/shard_map/reduce_scatter | solution.py:121
  580.5 1.0 add_convert_fusion
  581.4 0.8 copy.51
  (28 shorter events, 0.4 us)
Async XLA Ops:
  6.5 84.9 %all-gather.7.cloned.1.call-start = ((), (), s32[]{:S(2)}) async-start(), calls=%async_computation.2 | async-start | bytes 1671168 | tf_op jit(solution)/shard_map/all_gather | solution.py:111
  8.2 194.9 %all-gather.9.cloned.1.call-start = ((), (), s32[]{:S(2)}) async-start(), calls=%async_computation.3 | async-start | bytes 2433024 | tf_op jit(solution)/shard_map/all_gather | solution.py:66
  9.9 286.5 %reduce-scatter.3.cloned.1.call-start = ((), (), s32[]{:S(2)}) async-start(), calls=%async_computation.4 | async-start | bytes 1671168 | tf_op jit(solution)/shard_map/reduce_scatter | solution.py:114
  207.2 4.5 collective-permute-start
  209.4 8.0 %collective-permute-start.1 = (bf16[2,2,4,32,128]{4,3,2,1,0:T(8,128)(2,1)S(1)}, bf16[2,2,4,32,128]{4,3,2,1,0:T(8,128)(2,1)S(1)}, u32[]{:S(2)}, u32[]{:S(2)}) collective-permute-start(bf16[2,2,4,32,128]{4,3,2,1,0:T(8,128)(2,1)S(1)} %pad_maximum_fusion.2), channel_id=1, source_target_pairs={{16,0},{32,16},{48,32},{64,48},{80,64},{96,80},{112,96},{128,112},... | collective-permute-start | bytes 393224 | tf_op jit(solution)/shard_map/ppermute | solution.py:20
  218.0 78.4 %copy-start = (bf16[256,192]{0,1:T(8,128)(2,1)S(1)}, bf16[256,192]{0,1:T(8,128)(2,1)}, u32[]{:S(2)}) copy-start(bf16[256,192]{0,1:T(8,128)(2,1)} %copy.37) | copy-start | bytes 294916
  220.2 146.8 %all-gather.11.cloned.1.call-start = ((), (), s32[]{:S(2)}) async-start(), calls=%async_computation.5 | async-start | bytes 1671168 | tf_op jit(solution)/shard_map/all_gather | solution.py:118
  298.0 189.2 %all-gather.13.cloned.1.call-start = ((), (), s32[]{:S(2)}) async-start(), calls=%async_computation.6 | async-start | bytes 2433024 | tf_op jit(solution)/shard_map/all_gather | solution.py:66
  298.8 281.7 %reduce-scatter.5.cloned.1.call-start = ((), (), s32[]{:S(2)}) async-start(), calls=%async_computation.7 | async-start | bytes 1671168 | tf_op jit(solution)/shard_map/reduce_scatter | solution.py:121
  491.3 4.1 collective-permute-start.2
  493.5 8.0 %collective-permute-start.3 = (bf16[2,2,4,32,128]{4,3,2,1,0:T(8,128)(2,1)S(1)}, bf16[2,2,4,32,128]{4,3,2,1,0:T(8,128)(2,1)S(1)}, u32[]{:S(2)}, u32[]{:S(2)}) collective-permute-start(bf16[2,2,4,32,128]{4,3,2,1,0:T(8,128)(2,1)S(1)} %pad_maximum_fusion.3), channel_id=1, source_target_pairs={{16,0},{32,16},{48,32},{64,48},{80,64},{96,80},{112,96},{128,112},... | collective-permute-start | bytes 393224 | tf_op jit(solution)/shard_map/ppermute | solution.py:20
Sparse Core Ops, SparseCore 0:
  9.5 46.9 all-gather.6
  59.6 143.5 all-gather.8
  220.4 75.9 reduce-scatter.2
  298.6 42.7 all-gather.10
  344.9 142.3 all-gather.12
  504.4 75.9 reduce-scatter.4
where the time goes:
time: 591 us; the launch traced here: 589 us
  waiting for transfers between devices  393 us (66%)
  blocking collectives  141 us (24%)
  between operations  13.8 us (2%)
  matrix products  12.6 us (2%)
  other arithmetic  11 us (2%)
  local copies, waits for them, and re-layouts  10.7 us (2%)
  starting transfers between devices  7.16 us (1%)
    all_gather x2, waiting for transfers between devices, project_in(): lax.all_gather(local_weight, 'sp', axis=0, tiled=True)  228 us
    reduce_scatter x2, waiting for transfers between devices, on_device(): lax.psum_scatter(partial_value.astype(jnp.bfloat16), 'tp', scatter_dimens...  152 us
    all_gather x2, blocking collectives, project_out(): lax.all_gather(out_weight[which_block], 'sp', axis=1, tiled=True)  141 us
  transfers between devices with their start and end apart: 10, of which 7 were waited for; matrix products, arithmetic and copies ran while one was open for 3% of the time, Pallas kernels for 0%

commit v1 on v0

v1 whole, which is shorter than its diff:
```python
import functools
import math

import jax
import jax.numpy as jnp
from jax import lax
from jax.experimental import pallas as pl
from jax.experimental.pallas import tpu as pltpu
from jax.sharding import Mesh, PartitionSpec as P

WH = 4
WW = 8
TP = ("xl", "y", "c")
SP = ("z", "xh")
NT = (((1,), (1,)), ((), ()))
TN = (((0,), (0,)), ((), ()))


def head_attention(projected, row_scale, qk_gain, same_window):
    width = projected.shape[1] // 3

    def normed(part, which):
        rows = projected[:, part * width : (part + 1) * width] * row_scale
        mean_square = jnp.mean(rows * rows, axis=-1, keepdims=True)
        return (rows * lax.rsqrt(mean_square + 1e-06) * qk_gain[which : which + 1, :]).astype(
            jnp.bfloat16
        )

    queries, key_rows = normed(0, 0), normed(1, 1)
    value_rows = (projected[:, 2 * width :] * row_scale).astype(jnp.bfloat16)
    scores = lax.dot_general(queries, key_rows, NT, preferred_element_type=jnp.float32)
    weights = jnp.where(same_window, jnp.exp(scores * (1.0 / math.sqrt(width))), 0.0)
    weights = (weights / jnp.sum(weights, axis=-1, keepdims=True)).astype(jnp.bfloat16)
    return jnp.dot(weights, value_rows, preferred_element_type=jnp.float32).astype(jnp.bfloat16)


def block_kernel(
    slab_rows, half_cols, total_rows, total_cols,
    place, x_ref, w_ref, w2_ref, gain_ref, qk_gain_ref, out_ref, scaled_ref,
):
    width, tokens = x_ref.shape
    step = gain_ref.shape[1]
    gains = gain_ref[...].T
    squares = jnp.zeros((step, tokens), jnp.float32)
    for i in range(width // step):
        rows = x_ref[i * step : (i + 1) * step, :].astype(jnp.float32)
        squares = squares + rows * rows
        scaled_ref[:, i * step : (i + 1) * step] = (rows * gains[:, i : i + 1]).T.astype(
            jnp.bfloat16
        )
    mean_square = jnp.sum(squares, axis=0, keepdims=True) * (1.0 / width)
    row_scale = jnp.broadcast_to(lax.rsqrt(mean_square + 1e-06), (8, tokens)).T[:, 0:1]

    first_row, shift_row, shift_col, first_col = place[0], place[1], place[2], place[3]

    def window(axis):
        token = lax.broadcasted_iota(jnp.int32, (tokens, tokens), axis)
        col = first_col + lax.bitwise_and(token, half_cols - 1)
        row = lax.bitwise_and(
            lax.shift_right_logical(token, half_cols.bit_length() - 1), slab_rows - 1
        )
        row = lax.bitwise_and(first_row + row, total_rows - 1)
        col = jnp.where(col < shift_col, col + total_cols, col)
        row_window = lax.shift_right_logical(row + shift_row, WH.bit_length() - 1)
        return row_window * 16 + lax.shift_right_logical(col, WW.bit_length() - 1)

    same_window = window(0) == window(1)
    heads = []
    for ref in (w_ref, w2_ref):
        head = qk_gain_ref.shape[1]
        projected = jnp.dot(
            scaled_ref[...], ref[:, : 3 * head], preferred_element_type=jnp.float32
        )
        heads.append(head_attention(projected, row_scale, qk_gain_ref[...], same_window))
    chunk = 512
    for i in range(width // chunk):
        rows = slice(i * chunk, (i + 1) * chunk)
        total = jnp.zeros((chunk, tokens), jnp.float32)
        for ref, attended in zip((w_ref, w2_ref), heads):
            total = total + lax.dot_general(
                ref[rows, 3 * head :], attended, NT, preferred_element_type=jnp.float32
            )
        out_ref[rows, :] = total.astype(jnp.bfloat16)


def run_block(dims, place, x_t, w, w2, gain, qk_gain):
    width, tokens = x_t.shape
    vmem = pl.BlockSpec(memory_space=pltpu.VMEM)
    return pl.pallas_call(
        functools.partial(block_kernel, *dims),
        out_shape=jax.ShapeDtypeStruct((width, tokens), jnp.bfloat16),
        in_specs=[pl.BlockSpec(memory_space=pltpu.SMEM)] + [vmem] * 5,
        out_specs=vmem,
        scratch_shapes=[pltpu.VMEM((tokens, width), jnp.bfloat16)],
        compiler_params=pltpu.CompilerParams(vmem_limit_bytes=32 * 1024 * 1024),
        cost_estimate=pl.CostEstimate(
            flops=2 * tokens * width * 2 * w.shape[1],
            bytes_accessed=4 * width * w.shape[1] + 4 * width * tokens,
            transcendentals=2 * tokens * tokens,
        ),
        name="window_block",
    )(place, x_t, w, w2, gain, qk_gain)


def neighbour(x, distance):
    count = lax.axis_size(SP)
    return lax.ppermute(x, SP, [(i, (i - distance) % count) for i in range(count)])


def swap_cores(x):
    return lax.ppermute(x, "c", [(0, 1), (1, 0)])


def on_device(tokens, qkv_weight, out_weight, norm_gain, qk_gain, shifts):
    frames, slab_rows, cols, local = tokens.shape
    count = frames * slab_rows * cols
    half = count // 2
    half_cols = cols // 2
    tp_count = lax.axis_size(TP)
    width = local * tp_count
    head = qk_gain.shape[-1]
    total_rows = slab_rows * lax.axis_size(SP)
    sp_rank = lax.axis_index(SP)
    core = lax.axis_index("c")

    shard = jnp.concatenate(
        [
            part
            for b in range(2)
            for part in (qkv_weight[b].reshape(-1, 3 * head), out_weight[b].T)
        ],
        axis=1,
    )
    pair = lax.all_gather(shard, "xh", axis=0, tiled=True)
    gathered = lax.all_gather(pair, "z", axis=0, tiled=True)
    own = [gathered[:, b * 4 * head : (b + 1) * 4 * head] for b in range(2)]
    other = [swap_cores(w) for w in own]

    offset = [shifts[1, 0] + slab_rows // 2, shifts[1, 0]]
    lane = jnp.arange(count, dtype=jnp.int32)
    nat_f, nat_r, nat_w = lane // (slab_rows * cols), lane // cols % slab_rows, lane % cols
    pos_f = lane // (slab_rows * half_cols) % frames
    pos_r = lane // half_cols % slab_rows
    pos_j = lane // half * half_cols + lane % half_cols

    def pick(rows_f, rows_r, rows_c, f, r, c):
        hit = (rows_f[:, None] == f[None]) & (rows_r[:, None] == r[None])
        return (hit & (rows_c[:, None] == c[None])).astype(jnp.bfloat16)

    def place(b):
        first_row = slab_rows * sp_rank - offset[b] + total_rows
        return jnp.stack(
            [first_row, shifts[b, 0], shifts[b, 1], core * half_cols]
        ).astype(jnp.int32)

    dims = (slab_rows, half_cols, total_rows, cols)

    def block(x_t, b):
        pieces = jnp.stack([x_t[:, :half], x_t[:, half:]])
        pieces = jnp.broadcast_to(pieces[None], (tp_count // 2, 2, local, half))
        pieces = pieces.reshape(tp_count, local, half)
        full = lax.all_to_all(pieces, TP, 0, 0, tiled=True).reshape(width, half)
        partial_value = run_block(
            dims, place(b), full, own[b], other[b],
            norm_gain[b].reshape(-1, 128), qk_gain[b],
        )
        parts = lax.all_to_all(
            partial_value.reshape(tp_count, local, half), TP, 0, 0, tiled=True
        )
        parts = parts.reshape(tp_count // 2, 2, local, half).astype(jnp.float32)
        total = jnp.sum(parts, axis=0)
        total = jnp.concatenate([total[0], total[1]], axis=1)
        return (x_t.astype(jnp.float32) + total).astype(jnp.bfloat16)

    def exact(terms, dims_):
        total = sum(
            lax.dot_general(a, b, dims_, preferred_element_type=jnp.float32) for a, b in terms
        )
        return total.astype(jnp.bfloat16)

    natural = tokens.reshape(count, local)
    before = neighbour(natural, -1)
    last_row = neighbour(tokens[:, -1].reshape(frames * cols, local), -2)
    from_before = slab_rows - offset[0] + pos_r
    pos_w = (pos_j - shifts[0, 1]) % cols
    edge = jnp.arange(frames * cols, dtype=jnp.int32)
    x_t = exact(
        [
            (natural, pick(nat_f, nat_r, nat_w, pos_f, from_before - slab_rows, pos_w)),
            (before, pick(nat_f, nat_r, nat_w, pos_f, from_before, pos_w)),
            (last_row, pick(edge // cols, edge * 0 - 1, edge % cols, pos_f, from_before, pos_w)),
        ],
        TN,
    )
    x_t = block(x_t, 0)

    after = neighbour(x_t, 1)
    old_j = (pos_j - shifts[1, 1] + shifts[0, 1]) % cols
    moved = pos_r + slab_rows // 2
    nn = (((1,), (0,)), ((), ()))
    x_t = exact(
        [
            (x_t, pick(pos_f, pos_r, pos_j, pos_f, moved, old_j)),
            (after, pick(pos_f, pos_r, pos_j, pos_f, moved - slab_rows, old_j)),
        ],
        nn,
    )
    x_t = block(x_t, 1)

    after = neighbour(x_t, 1)
    new_j = (nat_w + shifts[1, 1]) % cols
    moved = nat_r + offset[1]
    result = exact(
        [
            (pick(nat_f, moved, new_j, pos_f, pos_r, pos_j), x_t),
            (pick(nat_f, moved - slab_rows, new_j, pos_f, pos_r, pos_j), after),
        ],
        NT,
    )
    return result.reshape(frames, slab_rows, cols, local)


def solution(mesh):
    shape = mesh.devices.shape
    fine = Mesh(mesh.devices.reshape(shape[0] // 2, 2, 2, shape[1] // 4, 2), SP + TP)
    placed = (
        P(None, SP, None, TP),
        P(None, SP, None, TP),
        P(None, TP, SP),
        P(),
        P(),
        P(),
    )
    return jax.shard_map(
        on_device, mesh=fine, in_specs=placed, out_specs=P(None, SP, None, TP), check_vma=False
    )
```

time: 591 us -> 246 us (0.42)
  waiting for transfers between devices: 393 us -> 141 us
  blocking collectives: 141 us -> 7.39 us
  starting transfers between devices: 7.16 us -> 45.8 us
  Pallas kernels: 0 us -> 11.8 us
  matrix products: 12.6 us -> 3.11 us
    reduce_scatter x2 -> x0, waiting for transfers between devices: 152 us -> none  [on_device(): lax.psum_scatter(partial_value.astype(jnp.bfloat16), 'tp', scatter_dimens...]
    all_gather x4 -> x1, waiting for transfers between devices: 228 us -> 91.1 us  [on_device(): gathered = lax.all_gather(pair, 'z', axis=0, tiled=True)]
    all_gather x2 -> x1, blocking collectives: 141 us -> 7.39 us  [on_device(): pair = lax.all_gather(shard, 'xh', axis=0, tiled=True)]
    all_to_all x0 -> x4, waiting for transfers between devices: none -> 45.3 us  [the longest x2 23.1 us: block(): lax.all_to_all(partial_value.reshape(tp_count, local, half), TP, 0, 0, ti...]
    all_to_all x0 -> x4, starting transfers between devices: none -> 21.5 us  [the longest x2 12.4 us: block(): full = lax.all_to_all(pieces, TP, 0, 0, tiled=True).reshape(width, half)]
    ppermute x4 -> x6, starting transfers between devices: 6.95 us -> 24.3 us  [the longest x4 17.5 us: neighbour(): lax.ppermute(x, SP, [(i, (i - distance) % count) for i in range(count)])]
    pallas_call x0 -> x2, Pallas kernels: none -> 11.8 us  [run_block(): pl.pallas_call(functools.partial(block_kernel, *dims), out_shape=jax.Shap...]
    dot_general x6 -> x7, matrix products: 12.6 us -> 3.11 us  [exact(): lax.dot_general(a, b, dims_, preferred_element_type=jnp.float32)]
  transfers between devices with their start and end apart: 10 -> 11, of which waited for: 7 -> 8; matrix products, arithmetic and copies ran while one was open for 3% -> 6% of each run, Pallas kernels for 0% -> 3%
where the time goes in v1:
time: 246 us; the launch traced here: 245 us
  waiting for transfers between devices  141 us (57%)
  starting transfers between devices  45.8 us (19%)
  between operations  15 us (6%)
  local copies, waits for them, and re-layouts  12.9 us (5%)
  Pallas kernels  11.8 us (5%)
  other arithmetic  7.78 us (3%)
  blocking collectives  7.39 us (3%)
  matrix products  3.11 us (1%)
    all_gather x1, waiting for transfers between devices, on_device(): gathered = lax.all_gather(pair, 'z', axis=0, tiled=True)  91.1 us
    all_to_all x2, waiting for transfers between devices, block(): lax.all_to_all(partial_value.reshape(tp_count, local, half), TP, 0, 0, ti...  23.1 us
    all_to_all x2, waiting for transfers between devices, block(): full = lax.all_to_all(pieces, TP, 0, 0, tiled=True).reshape(width, half)  22.2 us
    ppermute x4, starting transfers between devices, neighbour(): lax.ppermute(x, SP, [(i, (i - distance) % count) for i in range(count)])  17.5 us
    all_to_all x2, starting transfers between devices, block(): full = lax.all_to_all(pieces, TP, 0, 0, tiled=True).reshape(width, half)  12.4 us
    pallas_call x2, Pallas kernels, run_block(): pl.pallas_call(functools.partial(block_kernel, *dims), out_shape=jax.Shap...  11.8 us
    all_to_all x2, starting transfers between devices, block(): lax.all_to_all(partial_value.reshape(tp_count, local, half), TP, 0, 0, ti...  9.17 us
    all_gather x1, blocking collectives, on_device(): pair = lax.all_gather(shard, 'xh', axis=0, tiled=True)  7.39 us
  transfers between devices with their start and end apart: 11, of which 8 were waited for; matrix products, arithmetic and copies ran while one was open for 6% of the time, Pallas kernels for 3%

profile of v1, /device:TPU:1, one launch (start us, length us, event | category | flops | bytes accessed | tf_op | source)
XLA Modules:
  0.0 245.0 jit_solution(10619955435539568112)
XLA Ops:
  6.5 0.0 all-gather.2.cloned.1.call-start
  6.5 0.8 slice_bitcast_fusion.9
  7.3 0.9 fusion.73
  8.2 0.1 copy.11
  8.3 0.1 copy.10
  8.4 7.4 %all_gather.6 = bf16[192,1024]{1,0:T(8,128)(2,1)} all-gather(bf16[96,1024]{1,0:T(8,128)(2,1)S(1)} %pad_maximum_fusion), channel_id=1, replica_groups=mesh['z'=16,'xh'=2,'xl'=2,'y'=4,'c'=2] {'xh'}, dimensions={0}, use_global_device_ids=true | all-gather | bytes 589824 | tf_op jit(solution)/shard_map/all_gather | solution.py:134
  15.8 0.0 all-gather.2.cloned.1.call-update
  15.8 0.0 copy-start.3
  15.8 91.1 %all-gather.2.cloned.1.call-done = bf16[3072,1024]{1,0:T(8,128)(2,1)} async-done(((bf16[192,1024]{1,0:T(8,128)(2,1)}), bf16[3072,1024]{1,0:T(8,128)(2,1)}) %all-gather.2.cloned.1.call-update) | async-done | bytes 6291472 | tf_op jit(solution)/shard_map/all_gather | solution.py:135
  107.0 5.0 %fusion.72 = (bf16[3072,512]{1,0:T(8,128)(2,1)S(1)}, bf16[3072,512]{1,0:T(8,128)(2,1)}) fusion(bf16[3072,1024]{1,0:T(8,128)(2,1)} %all-gather.2.cloned.1.call-done), kind=kLoop, calls=%fused_computation.155 | loop fusion | bytes 12582912 | tf_op jit(solution)/shard_map/slice | solution.py:136
  111.9 0.0 copy-start.2
  111.9 0.0 copy-start.4
  111.9 4.7 %collective-permute-start.2 = (bf16[3072,512]{1,0:T(8,128)(2,1)}, bf16[3072,512]{1,0:T(8,128)(2,1)}, u32[]{:S(2)}, u32[]{:S(2)}) collective-permute-start(bf16[3072,512]{1,0:T(8,128)(2,1)} %get-tuple-element.6.w_ref), channel_id=1, source_target_pairs={{0,1},{1,0},{2,3},{3,2},{4,5},{5,4},{6,7},{7,6},{8,9},{9,8},{10,11... | collective-permute-start | bytes 9437192 | tf_op jit(solution)/shard_map/ppermute | solution.py:111
  116.7 0.8 slice.78
  117.4 2.2 collective-permute-start.1
  119.7 4.6 %collective-permute-start = (bf16[256,192]{1,0:T(8,128)(2,1)}, bf16[256,192]{1,0:T(8,128)(2,1)S(1)}, u32[]{:S(2)}, u32[]{:S(2)}) collective-permute-start(bf16[256,192]{1,0:T(8,128)(2,1)} %bitcast.3), channel_id=1, source_target_pairs={{0,16},{16,32},{32,48},{48,64},{64,80},{80,96},{96,112},{112,128},... | collective-permute-start | bytes 294920 | tf_op jit(solution)/shard_map/ppermute | solution.py:107
  124.3 0.0 copy-done.3
  124.3 0.6 fusion.75
  125.7 0.6 and_select_fusion.3
  126.2 1.2 fusion.6
  127.5 1.3 add_add_fusion.place
  128.8 0.0 collective-permute-done.1
  128.8 0.3 fusion.52
  129.1 1.1 collective-permute-done
  130.2 0.3 fusion.4
  130.6 1.0 broadcast_in_dim.4
  131.7 6.3 %all-to-all-start = ((bf16[16,192,128]{2,1,0:T(8,128)(2,1)}), bf16[16,192,128]{2,1,0:T(8,128)(2,1)}, u32[]{:S(2)}, u32[]{:S(2)}) async-start(bf16[16,192,128]{2,1,0:T(8,128)(2,1)} %bitcast.74), calls=%async_computation | async-start | bytes 1572864 | tf_op jit(solution)/shard_map/all_to_all | solution.py:162
  138.0 0.0 copy-done.2
  138.0 2.1 collective-permute-start.4
  140.1 0.0 copy-done.4
  140.1 11.0 %all-to-all-done = bf16[16,192,128]{2,1,0:T(8,128)(2,1)} async-done(((bf16[16,192,128]{2,1,0:T(8,128)(2,1)}), bf16[16,192,128]{2,1,0:T(8,128)(2,1)}, u32[]{:S(2)}, u32[]{:S(2)}) %all-to-all-start) | async-done | bytes 786464 | tf_op jit(solution)/shard_map/all_to_all | solution.py:162
  151.1 0.0 collective-permute-done.2.w2_ref
  151.1 6.4 %window_block.2 = bf16[3072,128]{1,0:T(8,128)(2,1)S(1)} custom-call(s32[4]{0:T(128)S(1)} %add_add_fusion.place, bf16[3072,128]{1,0:T(8,128)(2,1)} %bitcast.13.x_ref, bf16[3072,512]{1,0:T(8,128)(2,1)} %get-tuple-element.6.w_ref, bf16[3072,512]{1,0:T(8,128)(2,1)} %collective-permute-done.2.w2_ref, f32[24,128]{1,0:T(8,128)S(1)} %bitcast.73, ...), custom_call_target="tpu_custom_call" | custom-call | flops 805306368 | bytes 7864320 | tf_op jit(solution)/shard_map/window_block/pallas_call | solution.py:89
  157.4 0.0 copy-start
  157.4 0.9 copy-done
  158.3 4.9 %all-to-all-start.1 = ((bf16[16,192,128]{2,1,0:T(8,128)(2,1)}), bf16[16,192,128]{2,1,0:T(8,128)(2,1)}, u32[]{:S(2)}, u32[]{:S(2)}) async-start(bf16[16,192,128]{2,1,0:T(8,128)(2,1)} %bitcast.70), calls=%async_computation.1 | async-start | bytes 1572864 | tf_op jit(solution)/shard_map/all_to_all | solution.py:167
  163.3 1.2 and_select_fusion
  164.5 11.9 %all-to-all-done.1 = bf16[16,192,128]{2,1,0:T(8,128)(2,1)} async-done(((bf16[16,192,128]{2,1,0:T(8,128)(2,1)}), bf16[16,192,128]{2,1,0:T(8,128)(2,1)}, u32[]{:S(2)}, u32[]{:S(2)}) %all-to-all-start.1) | async-done | bytes 786464 | tf_op jit(solution)/shard_map/all_to_all | solution.py:167
  176.4 1.3 convert_reduce_fusion.1
  177.7 4.3 %collective-permute-start.3 = (bf16[192,256]{1,0:T(8,128)(2,1)S(1)}, bf16[192,256]{1,0:T(8,128)(2,1)S(1)}, u32[]{:S(2)}, u32[]{:S(2)}) collective-permute-start(bf16[192,256]{1,0:T(8,128)(2,1)S(1)} %fusion.14), channel_id=1, source_target_pairs={{0,496},{16,0},{32,16},{48,32},{64,48},{80,64},{96,80},{112,96},{1... | collective-permute-start | bytes 294920 | tf_op jit(solution)/shard_map/ppermute | solution.py:107
  182.0 0.3 fusion.7
  182.3 2.3 collective-permute-done.3
  184.6 0.3 fusion.2
  185.0 1.1 broadcast_in_dim.5
  186.0 6.0 %all-to-all-start.2 = ((bf16[16,192,128]{2,1,0:T(8,128)(2,1)}), bf16[16,192,128]{2,1,0:T(8,128)(2,1)}, u32[]{:S(2)}, u32[]{:S(2)}) async-start(bf16[16,192,128]{2,1,0:T(8,128)(2,1)} %bitcast.75), calls=%async_computation.2 | async-start | bytes 1572864 | tf_op jit(solution)/shard_map/all_to_all | solution.py:162
  192.7 1.3 add_add_fusion.1.place
  194.0 0.0 collective-permute-done.4.w2_ref
  194.0 11.2 %all-to-all-done.2 = bf16[16,192,128]{2,1,0:T(8,128)(2,1)} async-done(((bf16[16,192,128]{2,1,0:T(8,128)(2,1)}), bf16[16,192,128]{2,1,0:T(8,128)(2,1)}, u32[]{:S(2)}, u32[]{:S(2)}) %all-to-all-start.2) | async-done | bytes 786464 | tf_op jit(solution)/shard_map/all_to_all | solution.py:162
  205.2 5.4 %window_block.3 = bf16[3072,128]{1,0:T(8,128)(2,1)S(1)} custom-call(s32[4]{0:T(128)S(1)} %add_add_fusion.1.place, bf16[3072,128]{1,0:T(8,128)(2,1)} %bitcast.30.x_ref, bf16[3072,512]{1,0:T(8,128)(2,1)S(1)} %get-tuple-element.5.w_ref, bf16[3072,512]{1,0:T(8,128)(2,1)} %collective-permute-done.4.w2_ref, f32[24,128]{1,0:T(8,128)S(1)} %bitcast.72, ...), custom_call_target="tpu_custom_call" | custom-call | flops 805306368 | bytes 7864320 | tf_op jit(solution)/shard_map/window_block/pallas_call | solution.py:89
  210.7 0.0 copy-start.1
  210.7 0.9 copy-done.1
  211.6 4.3 %all-to-all-start.3 = ((bf16[16,192,128]{2,1,0:T(8,128)(2,1)}), bf16[16,192,128]{2,1,0:T(8,128)(2,1)S(1)}, u32[]{:S(2)}, u32[]{:S(2)}) async-start(bf16[16,192,128]{2,1,0:T(8,128)(2,1)} %bitcast.71), calls=%async_computation.3 | async-start | bytes 1572864 | tf_op jit(solution)/shard_map/all_to_all | solution.py:167
  215.8 0.6 broadcast_add_fusion.1
  216.5 1.3 and_select_fusion.5
  217.7 11.2 %all-to-all-done.3 = bf16[16,192,128]{2,1,0:T(8,128)(2,1)S(1)} async-done(((bf16[16,192,128]{2,1,0:T(8,128)(2,1)}), bf16[16,192,128]{2,1,0:T(8,128)(2,1)S(1)}, u32[]{:S(2)}, u32[]{:S(2)}) %all-to-all-start.3) | async-done | bytes 786464 | tf_op jit(solution)/shard_map/all_to_all | solution.py:167
  228.9 0.1 convert_reduce_fusion
  229.1 6.4 %collective-permute-start.5 = (bf16[192,256]{1,0:T(8,128)(2,1)S(1)}, bf16[192,256]{1,0:T(8,128)(2,1)S(1)}, u32[]{:S(2)}, u32[]{:S(2)}) collective-permute-start(bf16[192,256]{1,0:T(8,128)(2,1)S(1)} %fusion.15), channel_id=1, source_target_pairs={{0,496},{16,0},{32,16},{48,32},{64,48},{80,64},{96,80},{112,96},{1... | collective-permute-start | bytes 294920 | tf_op jit(solution)/shard_map/ppermute | solution.py:107
  235.4 0.3 fusion.5
  235.8 1.3 collective-permute-done.5
  237.1 0.3 fusion.3
  237.4 0.8 copy.12
  (19 shorter events, 0.2 us)
Async XLA Ops:
  6.5 100.4 %all-gather.2.cloned.1.call-start = ((), (), s32[]{:S(2)}) async-start(), calls=%async_computation.4 | async-start | bytes 6684672 | tf_op jit(solution)/shard_map/all_gather | solution.py:135
  15.8 108.5 %copy-start.3 = (s32[2,2]{1,0:T(2,128)S(1)}, s32[2,2]{1,0:T(2,128)}, u32[]{:S(2)}) copy-start(s32[2,2]{1,0:T(2,128)} %param.11) | copy-start | bytes 52
  111.9 26.0 %copy-start.2 = (f32[2,3072]{1,0:T(2,128)S(1)}, f32[2,3072]{1,0:T(2,128)}, u32[]{:S(2)}) copy-start(f32[2,3072]{1,0:T(2,128)} %param.9) | copy-start | bytes 73732
  111.9 28.1 %copy-start.4 = (f32[2,2,128]{2,1,0:T(2,128)S(1)}, f32[2,2,128]{2,1,0:T(2,128)}, u32[]{:S(2)}) copy-start(f32[2,2,128]{2,1,0:T(2,128)} %param.10) | copy-start | bytes 6148
  111.9 39.1 %collective-permute-start.2 = (bf16[3072,512]{1,0:T(8,128)(2,1)}, bf16[3072,512]{1,0:T(8,128)(2,1)}, u32[]{:S(2)}, u32[]{:S(2)}) collective-permute-start(bf16[3072,512]{1,0:T(8,128)(2,1)} %get-tuple-element.6.w_ref), channel_id=1, source_target_pairs={{0,1},{1,0},{2,3},{3,2},{4,5},{5,4},{6,7},{7,6},{8,9},{9,8},{10,11... | collective-permute-start | bytes 9437192 | tf_op jit(solution)/shard_map/ppermute | solution.py:111
  117.4 11.4 %collective-permute-start.1 = (bf16[64,192]{1,0:T(8,128)(2,1)S(1)}, bf16[64,192]{1,0:T(8,128)(2,1)S(1)}, u32[]{:S(2)}, u32[]{:S(2)}) collective-permute-start(bf16[64,192]{1,0:T(8,128)(2,1)S(1)} %bitcast.79), channel_id=1, source_target_pairs={{0,32},{16,48},{32,64},{48,80},{64,96},{80,112},{96,128},{112,144}... | collective-permute-start | bytes 73736 | tf_op jit(solution)/shard_map/ppermute | solution.py:107
  119.7 10.5 %collective-permute-start = (bf16[256,192]{1,0:T(8,128)(2,1)}, bf16[256,192]{1,0:T(8,128)(2,1)S(1)}, u32[]{:S(2)}, u32[]{:S(2)}) collective-permute-start(bf16[256,192]{1,0:T(8,128)(2,1)} %bitcast.3), channel_id=1, source_target_pairs={{0,16},{16,32},{32,48},{48,64},{64,80},{80,96},{96,112},{112,128},... | collective-permute-start | bytes 294920 | tf_op jit(solution)/shard_map/ppermute | solution.py:107
  131.7 19.4 %all-to-all-start = ((bf16[16,192,128]{2,1,0:T(8,128)(2,1)}), bf16[16,192,128]{2,1,0:T(8,128)(2,1)}, u32[]{:S(2)}, u32[]{:S(2)}) async-start(bf16[16,192,128]{2,1,0:T(8,128)(2,1)} %bitcast.74), calls=%async_computation | async-start | bytes 1572864 | tf_op jit(solution)/shard_map/all_to_all | solution.py:162
  138.0 56.0 %collective-permute-start.4 = (bf16[3072,512]{1,0:T(8,128)(2,1)S(1)}, bf16[3072,512]{1,0:T(8,128)(2,1)}, u32[]{:S(2)}, u32[]{:S(2)}) collective-permute-start(bf16[3072,512]{1,0:T(8,128)(2,1)S(1)} %get-tuple-element.5.w_ref), channel_id=1, source_target_pairs={{0,1},{1,0},{2,3},{3,2},{4,5},{5,4},{6,7},{7,6},{8,9},{9,8},{10,11... | collective-permute-start | bytes 9437192 | tf_op jit(solution)/shard_map/ppermute | solution.py:111
  157.4 0.9 copy-start
  158.3 18.1 %all-to-all-start.1 = ((bf16[16,192,128]{2,1,0:T(8,128)(2,1)}), bf16[16,192,128]{2,1,0:T(8,128)(2,1)}, u32[]{:S(2)}, u32[]{:S(2)}) async-start(bf16[16,192,128]{2,1,0:T(8,128)(2,1)} %bitcast.70), calls=%async_computation.1 | async-start | bytes 1572864 | tf_op jit(solution)/shard_map/all_to_all | solution.py:167
  177.7 6.9 %collective-permute-start.3 = (bf16[192,256]{1,0:T(8,128)(2,1)S(1)}, bf16[192,256]{1,0:T(8,128)(2,1)S(1)}, u32[]{:S(2)}, u32[]{:S(2)}) collective-permute-start(bf16[192,256]{1,0:T(8,128)(2,1)S(1)} %fusion.14), channel_id=1, source_target_pairs={{0,496},{16,0},{32,16},{48,32},{64,48},{80,64},{96,80},{112,96},{1... | collective-permute-start | bytes 294920 | tf_op jit(solution)/shard_map/ppermute | solution.py:107
  186.0 19.2 %all-to-all-start.2 = ((bf16[16,192,128]{2,1,0:T(8,128)(2,1)}), bf16[16,192,128]{2,1,0:T(8,128)(2,1)}, u32[]{:S(2)}, u32[]{:S(2)}) async-start(bf16[16,192,128]{2,1,0:T(8,128)(2,1)} %bitcast.75), calls=%async_computation.2 | async-start | bytes 1572864 | tf_op jit(solution)/shard_map/all_to_all | solution.py:162
  210.7 0.9 copy-start.1
  211.6 17.3 %all-to-all-start.3 = ((bf16[16,192,128]{2,1,0:T(8,128)(2,1)}), bf16[16,192,128]{2,1,0:T(8,128)(2,1)S(1)}, u32[]{:S(2)}, u32[]{:S(2)}) async-start(bf16[16,192,128]{2,1,0:T(8,128)(2,1)} %bitcast.71), calls=%async_computation.3 | async-start | bytes 1572864 | tf_op jit(solution)/shard_map/all_to_all | solution.py:167
  229.1 8.0 %collective-permute-start.5 = (bf16[192,256]{1,0:T(8,128)(2,1)S(1)}, bf16[192,256]{1,0:T(8,128)(2,1)S(1)}, u32[]{:S(2)}, u32[]{:S(2)}) collective-permute-start(bf16[192,256]{1,0:T(8,128)(2,1)S(1)} %fusion.15), channel_id=1, source_target_pairs={{0,496},{16,0},{32,16},{48,32},{64,48},{80,64},{96,80},{112,96},{1... | collective-permute-start | bytes 294920 | tf_op jit(solution)/shard_map/ppermute | solution.py:107
Sparse Core Ops, SparseCore 0:
  15.9 90.9 all-gather.1

commit v2 on v1

v2 whole, which is shorter than its diff:
```python
import functools
import math

import jax
import jax.numpy as jnp
from jax import lax
from jax.experimental import pallas as pl
from jax.experimental.pallas import tpu as pltpu
from jax.sharding import Mesh, PartitionSpec as P

WH = 4
WW = 8
TP = ("xl", "y", "c")
SP = ("z8", "z2", "xh")
NT = (((1,), (1,)), ((), ()))
TN = (((0,), (0,)), ((), ()))


def head_attention(projected, row_scale, qk_gain, same_window):
    width = projected.shape[1] // 3

    def normed(part, which):
        rows = projected[:, part * width : (part + 1) * width] * row_scale
        mean_square = jnp.mean(rows * rows, axis=-1, keepdims=True)
        return (rows * lax.rsqrt(mean_square + 1e-06) * qk_gain[which : which + 1, :]).astype(
            jnp.bfloat16
        )

    queries, key_rows = normed(0, 0), normed(1, 1)
    value_rows = (projected[:, 2 * width :] * row_scale).astype(jnp.bfloat16)
    scores = lax.dot_general(queries, key_rows, NT, preferred_element_type=jnp.float32)
    weights = jnp.where(same_window, jnp.exp(scores * (1.0 / math.sqrt(width))), 0.0)
    weights = (weights / jnp.sum(weights, axis=-1, keepdims=True)).astype(jnp.bfloat16)
    return jnp.dot(weights, value_rows, preferred_element_type=jnp.float32).astype(jnp.bfloat16)


def block_kernel(dims, heads, groups, place, key, x_ref, qk_gain_ref, *refs):
    slab_rows, half_cols, total_rows, total_cols = dims
    weights, (out_ref, x_rows_ref) = refs[: heads * groups], refs[heads * groups :]
    slabs, outer, inner, rows, tokens = x_ref.shape
    head = qk_gain_ref.shape[1]
    part = outer * inner * rows // groups
    per = inner // groups

    def window(first_row, axis):
        token = lax.broadcasted_iota(jnp.int32, (tokens, tokens), axis)
        col = key[2] + lax.bitwise_and(token, half_cols - 1)
        row = lax.bitwise_and(
            lax.shift_right_logical(token, half_cols.bit_length() - 1), slab_rows - 1
        )
        row = lax.bitwise_and(first_row + row, total_rows - 1)
        col = jnp.where(col < key[1], col + total_cols, col)
        row_window = lax.shift_right_logical(row + key[0], WH.bit_length() - 1)
        return row_window * 16 + lax.shift_right_logical(col, WW.bit_length() - 1)

    scales = []
    for slab in range(slabs):
        squares = jnp.zeros((rows, tokens), jnp.float32)
        for g in range(groups):
            for i in range(per):
                for o in range(outer):
                    where = i if per == inner else place[g]
                    block = x_ref[slab, o, where].astype(jnp.float32)
                    squares = squares + block * block
        mean_square = jnp.sum(squares, axis=0, keepdims=True) * (1.0 / (outer * inner * rows))
        scales.append(jnp.broadcast_to(lax.rsqrt(mean_square + 1e-06), (8, tokens)).T[:, 0:1])
    for slab in range(slabs):
        for g in range(groups):
            if per == inner:
                block = x_ref[slab].reshape(part, tokens)
            else:
                block = x_ref[slab, :, place[g]].reshape(part, tokens)
            x_rows_ref[slab * tokens : (slab + 1) * tokens, g * part : (g + 1) * part] = block.T

    attended = []
    for h in range(heads):
        projected = jnp.zeros((slabs * tokens, 3 * head), jnp.float32)
        for g in range(groups):
            projected = projected + jnp.dot(
                x_rows_ref[:, g * part : (g + 1) * part],
                weights[h * groups + g][:, : 3 * head],
                preferred_element_type=jnp.float32,
            )
        rows_of = []
        for slab in range(slabs):
            first_row = key[3 + slab]
            rows_of.append(
                head_attention(
                    projected[slab * tokens : (slab + 1) * tokens],
                    scales[slab],
                    qk_gain_ref[...],
                    window(first_row, 0) == window(first_row, 1),
                )
            )
        attended.append(jnp.concatenate(rows_of, axis=0) if slabs > 1 else rows_of[0])
    chunk = part // 2
    for g in range(groups):
        for piece in range(2):
            total = jnp.zeros((chunk, slabs * tokens), jnp.float32)
            for h in range(heads):
                total = total + lax.dot_general(
                    weights[h * groups + g][piece * chunk : (piece + 1) * chunk, 3 * head :],
                    attended[h],
                    NT,
                    preferred_element_type=jnp.float32,
                )
            total = total.astype(jnp.bfloat16)
            span = outer // 2
            for slab in range(slabs):
                block = total[:, slab * tokens : (slab + 1) * tokens]
                where = slice(piece * span, (piece + 1) * span)
                if per == inner:
                    out_ref[slab, where] = block.reshape(span, inner, rows, tokens)
                else:
                    out_ref[slab, where, place[g]] = block.reshape(span, rows, tokens)


def run_block(dims, place, key, x, qk_gain, weights):
    slabs, outer, inner, rows, tokens = x.shape
    heads, groups = len(weights), len(weights[0])
    flat = [w for of_head in weights for w in of_head]
    features = outer * inner * rows
    vmem = pl.BlockSpec(memory_space=pltpu.VMEM)
    smem = pl.BlockSpec(memory_space=pltpu.SMEM)
    return pl.pallas_call(
        functools.partial(block_kernel, dims, heads, groups),
        out_shape=jax.ShapeDtypeStruct(x.shape, jnp.bfloat16),
        in_specs=[smem, smem] + [vmem] * (2 + len(flat)),
        out_specs=vmem,
        scratch_shapes=[pltpu.VMEM((slabs * tokens, features), jnp.bfloat16)],
        compiler_params=pltpu.CompilerParams(vmem_limit_bytes=32 * 1024 * 1024),
        cost_estimate=pl.CostEstimate(
            flops=2 * slabs * tokens * features * heads * flat[0].shape[1],
            bytes_accessed=2 * sum(w.size for w in flat) + 4 * x.size,
            transcendentals=heads * slabs * tokens * tokens,
        ),
        name="window_block",
    )(place, key, x, qk_gain, *flat)


def neighbour(x, distance):
    count = lax.axis_size(SP)
    return lax.ppermute(x, SP, [(i, (i - distance) % count) for i in range(count)])


def swap_cores(x):
    return lax.ppermute(x, "c", [(0, 1), (1, 0)])


def on_device(tokens, qkv_weight, out_weight, norm_gain, qk_gain, shifts):
    frames, slab_rows, cols, local = tokens.shape
    count = frames * slab_rows * cols
    half = count // 2
    half_cols = cols // 2
    tp_count = lax.axis_size(TP)
    head = qk_gain.shape[-1]
    shard_rows = out_weight.shape[-1]
    z_pairs = lax.axis_size("z8")
    sp_count = lax.axis_size(SP)
    total_rows = slab_rows * sp_count
    sp_rank = lax.axis_index(SP)
    x_hi, z_odd, core = lax.axis_index("xh"), lax.axis_index("z2"), lax.axis_index("c")

    def shard(b):
        gain = lax.dynamic_slice_in_dim(norm_gain[b], sp_rank * shard_rows, shard_rows)
        scaled = qkv_weight[b].reshape(shard_rows, 3 * head).astype(jnp.float32) * gain[:, None]
        return jnp.concatenate([scaled.astype(jnp.bfloat16), out_weight[b].T], axis=1)

    turned = lax.ppermute(
        shard(0), ("xh", "c"), [(xh * 2 + c, c * 2 + xh) for xh in range(2) for c in range(2)]
    )
    mine = shard(1)
    theirs = lax.ppermute(mine, "xh", [(0, 1), (1, 0)])
    pair = jnp.where(
        x_hi == 0,
        jnp.concatenate([mine, theirs], axis=0),
        jnp.concatenate([theirs, mine], axis=0),
    )

    offset = [shifts[1, 0] + slab_rows // 2, shifts[1, 0]]
    lane = jnp.arange(count, dtype=jnp.int32)
    nat_f, nat_r, nat_w = lane // (slab_rows * cols), lane // cols % slab_rows, lane % cols
    pos_f = lane // (slab_rows * half_cols) % frames
    pos_r = lane // half_cols % slab_rows
    pos_j = lane // half * half_cols + lane % half_cols

    def pick(rows_f, rows_r, rows_c, f, r, c):
        hit = (rows_f[:, None] == f[None]) & (rows_r[:, None] == r[None])
        return (hit & (rows_c[:, None] == c[None])).astype(jnp.bfloat16)

    dims = (slab_rows, half_cols, total_rows, cols)

    def key(b, slabs):
        first = [slab_rows * slab - offset[b] + total_rows for slab in slabs]
        return jnp.stack([shifts[b, 0], shifts[b, 1], core * half_cols, *first]).astype(jnp.int32)

    def spread(x_t, copies):
        pieces = jnp.stack([x_t[:, :half], x_t[:, half:]])
        pieces = jnp.broadcast_to(pieces[None], (copies, 2, local, half))
        return pieces.reshape(copies * 2, local, half)

    def add_up(x_t, parts):
        parts = parts.reshape(-1, 2, local, half).astype(jnp.float32)
        total = jnp.sum(parts, axis=0)
        total = jnp.concatenate([total[0], total[1]], axis=1)
        return (x_t.astype(jnp.float32) + total).astype(jnp.bfloat16)

    def exact(terms, dims_):
        total = sum(
            lax.dot_general(a, b, dims_, preferred_element_type=jnp.float32) for a, b in terms
        )
        return total.astype(jnp.bfloat16)

    natural = tokens.reshape(count, local)
    before = neighbour(natural, -1)
    last_row = neighbour(tokens[:, -1].reshape(frames * cols, local), -2)
    from_before = slab_rows - offset[0] + pos_r
    pos_w = (pos_j - shifts[0, 1]) % cols
    edge = jnp.arange(frames * cols, dtype=jnp.int32)
    x_t = exact(
        [
            (natural, pick(nat_f, nat_r, nat_w, pos_f, from_before - slab_rows, pos_w)),
            (before, pick(nat_f, nat_r, nat_w, pos_f, from_before, pos_w)),
            (last_row, pick(edge // cols, edge * 0 - 1, edge % cols, pos_f, from_before, pos_w)),
        ],
        TN,
    )
    pieces = spread(x_t, tp_count)
    pieces, turned, pair = lax.optimization_barrier((pieces, turned, pair))
    full = lax.all_to_all(pieces, ("xh",) + TP, 0, 0, tiled=True)
    gathered = lax.all_gather(pair, ("z8", "z2"), axis=0, tiled=True)
    near = lax.all_gather(turned, "z8", axis=0, tiled=True)
    z_count = 2 * z_pairs
    far = lax.ppermute(
        near,
        ("z8", "z2", "c"),
        [(z * 2 + c, (z + 1 - 2 * c) % z_count * 2 + c) for z in range(z_count) for c in range(2)],
    )
    weights = [near, far, swap_cores(near), swap_cores(far)]
    place = jnp.stack(
        [z_odd * 2 + core, (1 - z_odd) * 2 + core, z_odd * 2 + 1 - core, (1 - z_odd) * 2 + 1 - core]
    ).astype(jnp.int32)
    slab = sp_rank - x_hi
    sums = run_block(
        dims, place, key(0, [slab, slab + 1]),
        full.reshape(2, z_pairs, 4, shard_rows, half), qk_gain[0], [weights],
    )
    parts = lax.all_to_all(
        sums.reshape(2 * tp_count, local, half), ("xh",) + TP, 0, 0, tiled=True
    )
    x_t = add_up(x_t, parts)

    after = neighbour(x_t, 1)
    old_j = (pos_j - shifts[1, 1] + shifts[0, 1]) % cols
    moved = pos_r + slab_rows // 2
    nn = (((1,), (0,)), ((), ()))
    x_t = exact(
        [
            (x_t, pick(pos_f, pos_r, pos_j, pos_f, moved, old_j)),
            (after, pick(pos_f, pos_r, pos_j, pos_f, moved - slab_rows, old_j)),
        ],
        nn,
    )
    full = lax.all_to_all(spread(x_t, tp_count // 2), TP, 0, 0, tiled=True)
    sums = run_block(
        dims, place, key(1, [sp_rank]),
        full.reshape(1, sp_count, 1, shard_rows, half), qk_gain[1],
        [[gathered], [swap_cores(gathered)]],
    )
    parts = lax.all_to_all(sums.reshape(tp_count, local, half), TP, 0, 0, tiled=True)
    x_t = add_up(x_t, parts)

    after = neighbour(x_t, 1)
    new_j = (nat_w + shifts[1, 1]) % cols
    moved = nat_r + offset[1]
    result = exact(
        [
            (pick(nat_f, moved, new_j, pos_f, pos_r, pos_j), x_t),
            (pick(nat_f, moved - slab_rows, new_j, pos_f, pos_r, pos_j), after),
        ],
        NT,
    )
    return result.reshape(frames, slab_rows, cols, local)


def solution(mesh):
    shape = mesh.devices.shape
    fine = Mesh(mesh.devices.reshape(shape[0] // 4, 2, 2, 2, shape[1] // 4, 2), SP + TP)
    placed = (
        P(None, SP, None, TP),
        P(None, SP, None, TP),
        P(None, TP, SP),
        P(),
        P(),
        P(),
    )
    return jax.shard_map(
        on_device, mesh=fine, in_specs=placed, out_specs=P(None, SP, None, TP), check_vma=False
    )
```

time: 246 us -> 204 us (0.83)
  waiting for transfers between devices: 141 us -> 57.4 us
  blocking collectives: 7.39 us -> 34.2 us
  starting transfers between devices: 45.8 us -> 67.2 us
  local copies, waits for them, and re-layouts: 12.9 us -> 9.82 us
    all_gather x1, waiting for transfers between devices: 91.1 us -> 0.02 us  [on_device(): gathered = lax.all_gather(pair, ('z8', 'z2'), axis=0, tiled=True)]
    all_gather x1, blocking collectives: 7.39 us -> 34.2 us  [on_device(): near = lax.all_gather(turned, 'z8', axis=0, tiled=True)]
    ppermute x0 -> x3, starting transfers between devices: none -> 13.2 us  [the longest x1 5.16 us: on_device(): lax.ppermute(shard(0), ('xh', 'c'), [(xh * 2 + c, c * 2 + xh) for xh in r...]
    ppermute x0 -> x3, waiting for transfers between devices: none -> 8.02 us  [the longest x1 8.02 us: on_device(): lax.ppermute(near, ('z8', 'z2', 'c'), [(z * 2 + c, (z + 1 - 2 * c) % z_co...]
    ppermute x2 -> x3, starting transfers between devices: 6.78 us -> 12.1 us  [swap_cores(): return lax.ppermute(x, 'c', [(0, 1), (1, 0)])]
    slice x6 -> x2, local copies, waits for them, and re-layouts: 6.68 us -> 1.44 us  [the longest x1 0.84 us: shard(): norm_gain[b]]
  transfers between devices with their start and end apart: 11 -> 15, of which waited for: 8 -> 7; matrix products, arithmetic and copies ran while one was open for 6% -> 7% of each run, Pallas kernels for 3% -> 2%
where the time goes in v2:
time: 204 us; the launch traced here: 203 us
  starting transfers between devices  67.2 us (33%)
  waiting for transfers between devices  57.4 us (28%)
  blocking collectives  34.2 us (17%)
  between operations  15 us (7%)
  Pallas kernels  9.86 us (5%)
  local copies, waits for them, and re-layouts  9.82 us (5%)
  other arithmetic  7.16 us (4%)
  matrix products  2.22 us (1%)
    all_gather x1, blocking collectives, on_device(): near = lax.all_gather(turned, 'z8', axis=0, tiled=True)  34.2 us
    ppermute x4, starting transfers between devices, neighbour(): lax.ppermute(x, SP, [(i, (i - distance) % count) for i in range(count)])  18.2 us
    all_to_all x1, waiting for transfers between devices, on_device(): lax.all_to_all(sums.reshape(2 * tp_count, local, half), ('xh',) + TP, 0,...  16.7 us
    ppermute x3, starting transfers between devices, swap_cores(): return lax.ppermute(x, 'c', [(0, 1), (1, 0)])  12.1 us
    all_to_all x1, waiting for transfers between devices, on_device(): lax.all_to_all(sums.reshape(tp_count, local, half), TP, 0, 0, tiled=True)  11.2 us
    all_to_all x1, waiting for transfers between devices, on_device(): full = lax.all_to_all(spread(x_t, tp_count // 2), TP, 0, 0, tiled=True)  11.2 us
    pallas_call x2, Pallas kernels, run_block(): pl.pallas_call(functools.partial(block_kernel, dims, heads, groups), out_...  9.86 us
    all_to_all x1, starting transfers between devices, on_device(): full = lax.all_to_all(pieces, ('xh',) + TP, 0, 0, tiled=True)  9.67 us
  transfers between devices with their start and end apart: 15, of which 7 were waited for; matrix products, arithmetic and copies ran while one was open for 7% of the time, Pallas kernels for 2%

profile of v2, /device:TPU:1, one launch (start us, length us, event | category | flops | bytes accessed | tf_op | source)
XLA Modules:
  0.0 202.9 jit_solution(15943358064914279853)
XLA Ops:
  6.5 0.8 slice.72
  7.4 4.4 %collective-permute-start.1 = (bf16[64,192]{1,0:T(8,128)(2,1)S(1)}, bf16[64,192]{1,0:T(8,128)(2,1)S(1)}, u32[]{:S(2)}, u32[]{:S(2)}) collective-permute-start(bf16[64,192]{1,0:T(8,128)(2,1)S(1)} %bitcast.88), channel_id=1, source_target_pairs={{0,32},{16,48},{32,64},{48,80},{64,96},{80,112},{96,128},{112,144}... | collective-permute-start | bytes 73736 | tf_op jit(solution)/shard_map/ppermute | solution.py:143
  11.7 4.7 %collective-permute-start = (bf16[256,192]{1,0:T(8,128)(2,1)}, bf16[256,192]{1,0:T(8,128)(2,1)S(1)}, u32[]{:S(2)}, u32[]{:S(2)}) collective-permute-start(bf16[256,192]{1,0:T(8,128)(2,1)} %bitcast.89), channel_id=1, source_target_pairs={{0,16},{16,32},{32,48},{48,64},{64,80},{80,96},{96,112},{112,128},... | collective-permute-start | bytes 294920 | tf_op jit(solution)/shard_map/ppermute | solution.py:143
  16.4 0.8 fusion.74
  17.3 0.9 slice_convert_fusion
  18.2 0.1 copy.11
  18.3 0.8 slice_bitcast_fusion.8
  19.1 0.1 dynamic-slice_bitcast_fusion
  19.2 0.1 fusion.16
  19.3 3.5 %collective-permute-start.3 = (bf16[96,512]{1,0:T(8,128)(2,1)S(1)}, bf16[96,512]{1,0:T(8,128)(2,1)S(1)}, u32[]{:S(2)}, u32[]{:S(2)}) collective-permute-start(bf16[96,512]{1,0:T(8,128)(2,1)S(1)} %pad_maximum_fusion.2), channel_id=1, source_target_pairs={{0,16},{16,0},{1,17},{17,1},{2,18},{18,2},{3,19},{19,3},{4,20},{20... | collective-permute-start | bytes 294920 | tf_op jit(solution)/shard_map/ppermute | solution.py:173
  22.8 0.1 copy.10
  22.9 0.1 fusion.17
  23.0 5.2 %collective-permute-start.2 = (bf16[96,512]{1,0:T(8,128)(2,1)S(1)}, bf16[96,512]{1,0:T(8,128)(2,1)S(1)}, u32[]{:S(2)}, u32[]{:S(2)}) collective-permute-start(bf16[96,512]{1,0:T(8,128)(2,1)S(1)} %pad_maximum_fusion.1), channel_id=1, source_target_pairs={{0,0},{1,16},{16,1},{17,17},{2,2},{3,18},{18,3},{19,19},{4,4},{5,2... | collective-permute-start | bytes 294920 | tf_op jit(solution)/shard_map/ppermute | solution.py:169
  28.2 0.6 fusion.75
  28.8 0.6 and_select_fusion.3
  30.0 0.3 fusion.6
  30.4 0.0 collective-permute-done.1
  30.4 0.3 fusion.54
  30.6 0.0 collective-permute-done
  30.7 0.4 fusion.4
  31.0 0.0 collective-permute-done.3
  31.0 0.7 maximum_select_fusion
  31.8 0.0 collective-permute-done.2
  31.8 1.5 broadcast_in_dim.4
  33.3 0.0 all-gather.2.cloned.1.call-update
  33.3 34.2 %all_gather.6.refs_0_ = bf16[768,512]{1,0:T(8,128)(2,1)S(1)} all-gather(bf16[96,512]{1,0:T(8,128)(2,1)S(1)} %collective-permute-done.2), channel_id=1, replica_groups=mesh['z8'=8,'z2'=2,'xh'=2,'xl'=2,'y'=4,'c'=2] {'z8'}, dimensions={0}, use_global_device_ids=true | all-gather | bytes 884736 | tf_op jit(solution)/shard_map/all_gather | solution.py:232
  67.6 4.6 %collective-permute-start.4 = (bf16[768,512]{1,0:T(8,128)(2,1)S(1)}, bf16[768,512]{1,0:T(8,128)(2,1)S(1)}, u32[]{:S(2)}, u32[]{:S(2)}) collective-permute-start(bf16[768,512]{1,0:T(8,128)(2,1)S(1)} %all_gather.6.refs_0_), channel_id=1, source_target_pairs={{0,32},{1,481},{32,64},{33,1},{64,96},{65,33},{96,128},{97,65},{12... | collective-permute-start | bytes 2359304 | tf_op jit(solution)/shard_map/ppermute | solution.py:234
  72.1 9.7 %all-to-all-start = ((bf16[32,192,128]{2,1,0:T(8,128)(2,1)}), bf16[32,192,128]{2,1,0:T(8,128)(2,1)S(1)}, u32[]{:S(2)}, u32[]{:S(2)}) async-start(bf16[32,192,128]{2,1,0:T(8,128)(2,1)} %bitcast.83), calls=%async_computation | async-start | bytes 3145728 | tf_op jit(solution)/shard_map/all_to_all | solution.py:230
  81.8 2.1 %collective-permute-start.5 = (bf16[768,512]{1,0:T(8,128)(2,1)S(1)}, bf16[768,512]{1,0:T(8,128)(2,1)}, u32[]{:S(2)}, u32[]{:S(2)}) collective-permute-start(bf16[768,512]{1,0:T(8,128)(2,1)S(1)} %all_gather.6.refs_0_), channel_id=1, source_target_pairs={{0,1},{1,0},{2,3},{3,2},{4,5},{5,4},{6,7},{7,6},{8,9},{9,8},{10,11... | collective-permute-start | bytes 2359304 | tf_op jit(solution)/shard_map/ppermute | solution.py:147
  84.0 8.0 %collective-permute-done.4.refs_1_ = bf16[768,512]{1,0:T(8,128)(2,1)S(1)} collective-permute-done((bf16[768,512]{1,0:T(8,128)(2,1)S(1)}, bf16[768,512]{1,0:T(8,128)(2,1)S(1)}, u32[]{:S(2)}, u32[]{:S(2)}) %collective-permute-start.4) | collective-permute-done | bytes 786464 | tf_op jit(solution)/shard_map/ppermute | solution.py:234
  92.0 5.2 %collective-permute-start.6 = (bf16[768,512]{1,0:T(8,128)(2,1)S(1)}, bf16[768,512]{1,0:T(8,128)(2,1)}, u32[]{:S(2)}, u32[]{:S(2)}) collective-permute-start(bf16[768,512]{1,0:T(8,128)(2,1)S(1)} %collective-permute-done.4.refs_1_), channel_id=1, source_target_pairs={{0,1},{1,0},{2,3},{3,2},{4,5},{5,4},{6,7},{7,6},{8,9},{9,8},{10,11... | collective-permute-start | bytes 2359304 | tf_op jit(solution)/shard_map/ppermute | solution.py:147
  97.2 1.2 stack.60.key
  98.5 0.1 pad_add_fusion.place
  98.6 0.0 collective-permute-done.5.refs_2_
  98.6 5.9 %all-to-all-done = bf16[32,192,128]{2,1,0:T(8,128)(2,1)S(1)} async-done(((bf16[32,192,128]{2,1,0:T(8,128)(2,1)}), bf16[32,192,128]{2,1,0:T(8,128)(2,1)S(1)}, u32[]{:S(2)}, u32[]{:S(2)}) %all-to-all-start) | async-done | bytes 1572896 | tf_op jit(solution)/shard_map/all_to_all | solution.py:230
  104.5 0.0 collective-permute-done.6.refs_3_
  104.5 4.8 %window_block.2 = bf16[2,8,4,96,128]{4,3,2,1,0:T(8,128)(2,1)} custom-call(s32[4]{0:T(128)S(1)} %pad_add_fusion.place, s32[5]{0:T(128)S(1)} %stack.60.key, bf16[2,8,4,96,128]{4,3,2,1,0:T(8,128)(2,1)S(1)} %bitcast.81, f32[2,128]{1,0:T(2,128)S(1)} %get-tuple-element.26.qk_gain_ref, bf16[768,512]{1,0:T(8,128)(2,1)S(1)} %all_gather.6.refs_0_, ...), custom_call_target="tpu_custom_call" | custom-call | flops 805306368 | bytes 6291456 | tf_op jit(solution)/shard_map/window_block/pallas_call | solution.py:125
  109.3 4.4 %all-to-all-start.1 = ((bf16[32,192,128]{2,1,0:T(8,128)(2,1)}), bf16[32,192,128]{2,1,0:T(8,128)(2,1)S(1)}, u32[]{:S(2)}, u32[]{:S(2)}) async-start(bf16[32,192,128]{2,1,0:T(8,128)(2,1)} %bitcast.26), calls=%async_computation.1 | async-start | bytes 3145728 | tf_op jit(solution)/shard_map/all_to_all | solution.py:248
  113.7 0.0 all-gather.2.cloned.1.call-done.refs_0_
  113.7 4.8 %collective-permute-start.8 = (bf16[3072,512]{1,0:T(8,128)(2,1)}, bf16[3072,512]{1,0:T(8,128)(2,1)}, u32[]{:S(2)}, u32[]{:S(2)}) collective-permute-start(bf16[3072,512]{1,0:T(8,128)(2,1)} %all-gather.2.cloned.1.call-done.refs_0_), channel_id=1, source_target_pairs={{0,1},{1,0},{2,3},{3,2},{4,5},{5,4},{6,7},{7,6},{8,9},{9,8},{10,11... | collective-permute-start | bytes 9437192 | tf_op jit(solution)/shard_map/ppermute | solution.py:147
  118.5 1.1 and_select_fusion
  119.6 16.7 %all-to-all-done.1 = bf16[32,192,128]{2,1,0:T(8,128)(2,1)S(1)} async-done(((bf16[32,192,128]{2,1,0:T(8,128)(2,1)}), bf16[32,192,128]{2,1,0:T(8,128)(2,1)S(1)}, u32[]{:S(2)}, u32[]{:S(2)}) %all-to-all-start.1) | async-done | bytes 1572896 | tf_op jit(solution)/shard_map/all_to_all | solution.py:248
  136.4 0.2 convert_reduce_fusion
  136.6 3.6 %collective-permute-start.7 = (bf16[192,256]{1,0:T(8,128)(2,1)S(1)}, bf16[192,256]{1,0:T(8,128)(2,1)S(1)}, u32[]{:S(2)}, u32[]{:S(2)}) collective-permute-start(bf16[192,256]{1,0:T(8,128)(2,1)S(1)} %fusion.14), channel_id=1, source_target_pairs={{0,496},{16,0},{32,16},{48,32},{64,48},{80,64},{96,80},{112,96},{1... | collective-permute-start | bytes 294920 | tf_op jit(solution)/shard_map/ppermute | solution.py:143
  140.3 0.3 fusion.7
  140.6 2.9 %collective-permute-done.7 = bf16[192,256]{1,0:T(8,128)(2,1)S(1)} collective-permute-done((bf16[192,256]{1,0:T(8,128)(2,1)S(1)}, bf16[192,256]{1,0:T(8,128)(2,1)S(1)}, u32[]{:S(2)}, u32[]{:S(2)}) %collective-permute-start.7) | collective-permute-done | bytes 98336 | tf_op jit(solution)/shard_map/ppermute | solution.py:143
  143.5 0.3 fusion.2
  143.9 1.0 broadcast_in_dim.5
  144.9 5.2 %all-to-all-start.2 = ((bf16[16,192,128]{2,1,0:T(8,128)(2,1)}), bf16[16,192,128]{2,1,0:T(8,128)(2,1)S(1)}, u32[]{:S(2)}, u32[]{:S(2)}) async-start(bf16[16,192,128]{2,1,0:T(8,128)(2,1)} %bitcast.35), calls=%async_computation.2 | async-start | bytes 1572864 | tf_op jit(solution)/shard_map/all_to_all | solution.py:264
  150.8 1.3 pad_add_fusion.1.key
  152.0 11.2 %all-to-all-done.2 = bf16[16,192,128]{2,1,0:T(8,128)(2,1)S(1)} async-done(((bf16[16,192,128]{2,1,0:T(8,128)(2,1)}), bf16[16,192,128]{2,1,0:T(8,128)(2,1)S(1)}, u32[]{:S(2)}, u32[]{:S(2)}) %all-to-all-start.2) | async-done | bytes 786464 | tf_op jit(solution)/shard_map/all_to_all | solution.py:264
  163.2 0.0 collective-permute-done.8.refs_1_
  163.2 1.9 copy-done
  165.1 5.1 %window_block.3 = bf16[1,32,1,96,128]{4,3,2,1,0:T(8,128)(2,1)} custom-call(s32[4]{0:T(128)S(1)} %pad_add_fusion.place, s32[4]{0:T(128)S(1)} %pad_add_fusion.1.key, bf16[1,32,1,96,128]{4,3,2,1,0:T(8,128)(2,1)S(1)} %bitcast.82, f32[2,128]{1,0:T(2,128)S(1)} %get-tuple-element.25.qk_gain_ref, bf16[3072,512]{1,0:T(8,128)(2,1)S(1)} %copy-done, ...), custom_call_target="tpu_custom_call" | custom-call | flops 805306368 | bytes 7864320 | tf_op jit(solution)/shard_map/window_block/pallas_call | solution.py:125
  170.2 4.3 %all-to-all-start.3 = ((bf16[16,192,128]{2,1,0:T(8,128)(2,1)}), bf16[16,192,128]{2,1,0:T(8,128)(2,1)S(1)}, u32[]{:S(2)}, u32[]{:S(2)}) async-start(bf16[16,192,128]{2,1,0:T(8,128)(2,1)} %bitcast.38), calls=%async_computation.3 | async-start | bytes 1572864 | tf_op jit(solution)/shard_map/all_to_all | solution.py:270
  174.5 0.6 broadcast_add_fusion.1
  175.1 1.2 and_select_fusion.5
  176.3 11.2 %all-to-all-done.3 = bf16[16,192,128]{2,1,0:T(8,128)(2,1)S(1)} async-done(((bf16[16,192,128]{2,1,0:T(8,128)(2,1)}), bf16[16,192,128]{2,1,0:T(8,128)(2,1)S(1)}, u32[]{:S(2)}, u32[]{:S(2)}) %all-to-all-start.3) | async-done | bytes 786464 | tf_op jit(solution)/shard_map/all_to_all | solution.py:270
  187.5 0.1 convert_reduce_fusion.1
  187.7 5.6 %collective-permute-start.9 = (bf16[192,256]{1,0:T(8,128)(2,1)S(1)}, bf16[192,256]{1,0:T(8,128)(2,1)S(1)}, u32[]{:S(2)}, u32[]{:S(2)}) collective-permute-start(bf16[192,256]{1,0:T(8,128)(2,1)S(1)} %fusion.15), channel_id=1, source_target_pairs={{0,496},{16,0},{32,16},{48,32},{64,48},{80,64},{96,80},{112,96},{1... | collective-permute-start | bytes 294920 | tf_op jit(solution)/shard_map/ppermute | solution.py:143
  193.3 0.3 fusion.5
  193.7 1.3 collective-permute-done.9
  195.0 0.3 fusion.3
  195.3 0.8 copy.12
  (26 shorter events, 0.2 us)
Async XLA Ops:
  6.5 23.4 %copy-start.1 = (bf16[2,4,32,192]{3,2,1,0:T(8,128)(2,1)S(1)}, bf16[2,4,32,192]{3,2,1,0:T(8,128)(2,1)}, u32[]{:S(2)}) copy-start(bf16[2,4,32,192]{3,2,1,0:T(8,128)(2,1)} %param.6) | copy-start | bytes 294916
  6.5 21.6 %copy-start.2 = (s32[2,2]{1,0:T(2,128)S(1)}, s32[2,2]{1,0:T(2,128)}, u32[]{:S(2)}) copy-start(s32[2,2]{1,0:T(2,128)} %param.11) | copy-start | bytes 52
  6.5 107.2 %all-gather.2.cloned.1.call-start = ((), (), s32[]{:S(2)}) async-start(), calls=%async_computation.4 | async-start | bytes 3342336 | tf_op jit(solution)/shard_map/all_gather | solution.py:231
  7.4 23.0 %collective-permute-start.1 = (bf16[64,192]{1,0:T(8,128)(2,1)S(1)}, bf16[64,192]{1,0:T(8,128)(2,1)S(1)}, u32[]{:S(2)}, u32[]{:S(2)}) collective-permute-start(bf16[64,192]{1,0:T(8,128)(2,1)S(1)} %bitcast.88), channel_id=1, source_target_pairs={{0,32},{16,48},{32,64},{48,80},{64,96},{80,112},{96,128},{112,144}... | collective-permute-start | bytes 73736 | tf_op jit(solution)/shard_map/ppermute | solution.py:143
  11.7 18.9 %collective-permute-start = (bf16[256,192]{1,0:T(8,128)(2,1)}, bf16[256,192]{1,0:T(8,128)(2,1)S(1)}, u32[]{:S(2)}, u32[]{:S(2)}) collective-permute-start(bf16[256,192]{1,0:T(8,128)(2,1)} %bitcast.89), channel_id=1, source_target_pairs={{0,16},{16,32},{32,48},{48,64},{64,80},{80,96},{96,112},{112,128},... | collective-permute-start | bytes 294920 | tf_op jit(solution)/shard_map/ppermute | solution.py:143
  19.3 11.8 %collective-permute-start.3 = (bf16[96,512]{1,0:T(8,128)(2,1)S(1)}, bf16[96,512]{1,0:T(8,128)(2,1)S(1)}, u32[]{:S(2)}, u32[]{:S(2)}) collective-permute-start(bf16[96,512]{1,0:T(8,128)(2,1)S(1)} %pad_maximum_fusion.2), channel_id=1, source_target_pairs={{0,16},{16,0},{1,17},{17,1},{2,18},{18,2},{3,19},{19,3},{4,20},{20... | collective-permute-start | bytes 294920 | tf_op jit(solution)/shard_map/ppermute | solution.py:173
  23.0 8.8 %collective-permute-start.2 = (bf16[96,512]{1,0:T(8,128)(2,1)S(1)}, bf16[96,512]{1,0:T(8,128)(2,1)S(1)}, u32[]{:S(2)}, u32[]{:S(2)}) collective-permute-start(bf16[96,512]{1,0:T(8,128)(2,1)S(1)} %pad_maximum_fusion.1), channel_id=1, source_target_pairs={{0,0},{1,16},{16,1},{17,17},{2,2},{3,18},{18,3},{19,19},{4,4},{5,2... | collective-permute-start | bytes 294920 | tf_op jit(solution)/shard_map/ppermute | solution.py:169
  67.5 31.0 %copy-start.3 = (f32[2,2,128]{2,1,0:T(2,128)S(1)}, f32[2,2,128]{2,1,0:T(2,128)}, u32[]{:S(2)}) copy-start(f32[2,2,128]{2,1,0:T(2,128)} %param.10) | copy-start | bytes 6148
  67.6 24.4 %collective-permute-start.4 = (bf16[768,512]{1,0:T(8,128)(2,1)S(1)}, bf16[768,512]{1,0:T(8,128)(2,1)S(1)}, u32[]{:S(2)}, u32[]{:S(2)}) collective-permute-start(bf16[768,512]{1,0:T(8,128)(2,1)S(1)} %all_gather.6.refs_0_), channel_id=1, source_target_pairs={{0,32},{1,481},{32,64},{33,1},{64,96},{65,33},{96,128},{97,65},{12... | collective-permute-start | bytes 2359304 | tf_op jit(solution)/shard_map/ppermute | solution.py:234
  72.1 32.4 %all-to-all-start = ((bf16[32,192,128]{2,1,0:T(8,128)(2,1)}), bf16[32,192,128]{2,1,0:T(8,128)(2,1)S(1)}, u32[]{:S(2)}, u32[]{:S(2)}) async-start(bf16[32,192,128]{2,1,0:T(8,128)(2,1)} %bitcast.83), calls=%async_computation | async-start | bytes 3145728 | tf_op jit(solution)/shard_map/all_to_all | solution.py:230
  81.8 16.8 %collective-permute-start.5 = (bf16[768,512]{1,0:T(8,128)(2,1)S(1)}, bf16[768,512]{1,0:T(8,128)(2,1)}, u32[]{:S(2)}, u32[]{:S(2)}) collective-permute-start(bf16[768,512]{1,0:T(8,128)(2,1)S(1)} %all_gather.6.refs_0_), channel_id=1, source_target_pairs={{0,1},{1,0},{2,3},{3,2},{4,5},{5,4},{6,7},{7,6},{8,9},{9,8},{10,11... | collective-permute-start | bytes 2359304 | tf_op jit(solution)/shard_map/ppermute | solution.py:147
  92.0 12.5 %collective-permute-start.6 = (bf16[768,512]{1,0:T(8,128)(2,1)S(1)}, bf16[768,512]{1,0:T(8,128)(2,1)}, u32[]{:S(2)}, u32[]{:S(2)}) collective-permute-start(bf16[768,512]{1,0:T(8,128)(2,1)S(1)} %collective-permute-done.4.refs_1_), channel_id=1, source_target_pairs={{0,1},{1,0},{2,3},{3,2},{4,5},{5,4},{6,7},{7,6},{8,9},{9,8},{10,11... | collective-permute-start | bytes 2359304 | tf_op jit(solution)/shard_map/ppermute | solution.py:147
  109.3 27.1 %all-to-all-start.1 = ((bf16[32,192,128]{2,1,0:T(8,128)(2,1)}), bf16[32,192,128]{2,1,0:T(8,128)(2,1)S(1)}, u32[]{:S(2)}, u32[]{:S(2)}) async-start(bf16[32,192,128]{2,1,0:T(8,128)(2,1)} %bitcast.26), calls=%async_computation.1 | async-start | bytes 3145728 | tf_op jit(solution)/shard_map/all_to_all | solution.py:248
  113.7 49.5 %collective-permute-start.8 = (bf16[3072,512]{1,0:T(8,128)(2,1)}, bf16[3072,512]{1,0:T(8,128)(2,1)}, u32[]{:S(2)}, u32[]{:S(2)}) collective-permute-start(bf16[3072,512]{1,0:T(8,128)(2,1)} %all-gather.2.cloned.1.call-done.refs_0_), channel_id=1, source_target_pairs={{0,1},{1,0},{2,3},{3,2},{4,5},{5,4},{6,7},{7,6},{8,9},{9,8},{10,11... | collective-permute-start | bytes 9437192 | tf_op jit(solution)/shard_map/ppermute | solution.py:147
  136.6 6.9 %collective-permute-start.7 = (bf16[192,256]{1,0:T(8,128)(2,1)S(1)}, bf16[192,256]{1,0:T(8,128)(2,1)S(1)}, u32[]{:S(2)}, u32[]{:S(2)}) collective-permute-start(bf16[192,256]{1,0:T(8,128)(2,1)S(1)} %fusion.14), channel_id=1, source_target_pairs={{0,496},{16,0},{32,16},{48,32},{64,48},{80,64},{96,80},{112,96},{1... | collective-permute-start | bytes 294920 | tf_op jit(solution)/shard_map/ppermute | solution.py:143
  144.9 18.3 %all-to-all-start.2 = ((bf16[16,192,128]{2,1,0:T(8,128)(2,1)}), bf16[16,192,128]{2,1,0:T(8,128)(2,1)S(1)}, u32[]{:S(2)}, u32[]{:S(2)}) async-start(bf16[16,192,128]{2,1,0:T(8,128)(2,1)} %bitcast.35), calls=%async_computation.2 | async-start | bytes 1572864 | tf_op jit(solution)/shard_map/all_to_all | solution.py:264
  163.2 1.9 copy-start
  170.2 17.3 %all-to-all-start.3 = ((bf16[16,192,128]{2,1,0:T(8,128)(2,1)}), bf16[16,192,128]{2,1,0:T(8,128)(2,1)S(1)}, u32[]{:S(2)}, u32[]{:S(2)}) async-start(bf16[16,192,128]{2,1,0:T(8,128)(2,1)} %bitcast.38), calls=%async_computation.3 | async-start | bytes 1572864 | tf_op jit(solution)/shard_map/all_to_all | solution.py:270
  187.7 7.3 %collective-permute-start.9 = (bf16[192,256]{1,0:T(8,128)(2,1)S(1)}, bf16[192,256]{1,0:T(8,128)(2,1)S(1)}, u32[]{:S(2)}, u32[]{:S(2)}) collective-permute-start(bf16[192,256]{1,0:T(8,128)(2,1)S(1)} %fusion.15), channel_id=1, source_target_pairs={{0,496},{16,0},{32,16},{48,32},{64,48},{80,64},{96,80},{112,96},{1... | collective-permute-start | bytes 294920 | tf_op jit(solution)/shard_map/ppermute | solution.py:143
Sparse Core Ops, SparseCore 0:
  33.5 75.5 all-gather.1

commit v3 on v2

v3 whole, which is shorter than its diff:
```python
import functools
import math

import jax
import jax.numpy as jnp
from jax import lax
from jax.experimental import pallas as pl
from jax.experimental.pallas import tpu as pltpu
from jax.sharding import Mesh, PartitionSpec as P

WH = 4
WW = 8
UNITS = 4
CHUNKS = 4
TP = ("xl", "y", "c")
SP = ("z8", "z2", "xh")
NT = (((1,), (1,)), ((), ()))
TN = (((0,), (0,)), ((), ()))


def head_attention(projected, row_scale, qk_gain, same_window):
    width = projected.shape[1] // 3

    def normed(part, which):
        rows = projected[:, part * width : (part + 1) * width] * row_scale
        mean_square = jnp.mean(rows * rows, axis=-1, keepdims=True)
        return (rows * lax.rsqrt(mean_square + 1e-06) * qk_gain[which : which + 1, :]).astype(
            jnp.bfloat16
        )

    queries, key_rows = normed(0, 0), normed(1, 1)
    value_rows = (projected[:, 2 * width :] * row_scale).astype(jnp.bfloat16)
    scores = lax.dot_general(queries, key_rows, NT, preferred_element_type=jnp.float32)
    weights = jnp.where(same_window, jnp.exp(scores * (1.0 / math.sqrt(width))), 0.0)
    weights = (weights / jnp.sum(weights, axis=-1, keepdims=True)).astype(jnp.bfloat16)
    return jnp.dot(weights, value_rows, preferred_element_type=jnp.float32).astype(jnp.bfloat16)


def block_kernel(spec, weights_are_pairs, shifts, x_ref, qk_gain_ref, *refs):
    copies = []
    if weights_are_pairs:
        source, out_ref, x_rows_ref, held_ref, sems = refs
        weights = [held_ref]
        size = source.shape[0] // CHUNKS
        for h in range(source.shape[1]):
            for n in range(CHUNKS):
                there = slice(n * size, (n + 1) * size)
                copies.append(
                    pltpu.make_async_copy(
                        source.at[there, h], held_ref.at[there, h], sems.at[h * CHUNKS + n]
                    )
                )
                copies[-1].start()
    else:
        weights, (out_ref, x_rows_ref) = refs[:-2], refs[-2:]
    slabs, units, rows, tokens = out_ref.shape
    heads = spec.heads
    windows = spec.windows
    head = qk_gain_ref.shape[1]
    step = UNITS * rows
    part = units // (CHUNKS if weights_are_pairs else len(weights))
    order = spec.order()
    shift_row, shift_col = shifts[spec.block, 0], shifts[spec.block, 1]
    first_rows = spec.first_rows(shifts)
    first_col = lax.axis_index("c") * spec.half_cols

    def weight(h, u, count, columns):
        if weights_are_pairs:
            per = weights[0].shape[2] // rows
            found = weights[0][u // per : (u + count) // per, h, :, columns]
            return found.reshape(count * rows, found.shape[-1])
        g, start = u // part, u % part * rows
        return weights[g][start : start + count * rows, columns]

    def window(first_row, axis):
        token = lax.broadcasted_iota(jnp.int32, (tokens, tokens), axis)
        col = first_col + lax.bitwise_and(token, spec.half_cols - 1)
        row = lax.bitwise_and(
            lax.shift_right_logical(token, spec.half_cols.bit_length() - 1), spec.slab_rows - 1
        )
        row = lax.bitwise_and(first_row + row, spec.total_rows - 1)
        col = jnp.where(col < shift_col, col + spec.total_cols, col)
        row_window = lax.shift_right_logical(row + shift_row, WH.bit_length() - 1)
        return row_window * 16 + lax.shift_right_logical(col, WW.bit_length() - 1)

    scales = []
    for w in range(windows):
        squares = jnp.zeros((rows, tokens), jnp.float32)
        for k in range(units):
            block = x_ref[spec.unit(w, k)].astype(jnp.float32)
            squares = squares + block * block
        mean_square = jnp.sum(squares, axis=0, keepdims=True) * (1.0 / (units * rows))
        scales.append(jnp.broadcast_to(lax.rsqrt(mean_square + 1e-06), (8, tokens)).T[:, 0:1])
        for u in range(0, units, UNITS):
            block = jnp.concatenate(
                [x_ref[spec.unit(w, order[u + k])] for k in range(UNITS)], axis=0
            )
            x_rows_ref[w * tokens : (w + 1) * tokens, u * rows : u * rows + step] = block.T

    attended = []
    for h in range(heads):
        projected = jnp.zeros((windows * tokens, 3 * head), jnp.float32)
        for u in range(0, units, part):
            if copies:
                copies[h * CHUNKS + u // part].wait()
            projected = projected + jnp.dot(
                x_rows_ref[:, u * rows : (u + part) * rows],
                weight(h, u, part, slice(0, 3 * head)),
                preferred_element_type=jnp.float32,
            )
        of_window = []
        for w in range(windows):
            first_row = first_rows[w]
            of_window.append(
                head_attention(
                    projected[w * tokens : (w + 1) * tokens],
                    scales[w],
                    qk_gain_ref[...],
                    window(first_row, 0) == window(first_row, 1),
                )
            )
        if windows > slabs:
            frame = tokens // spec.frames
            of_window = [
                of_window[s + (q % 2)][
                    q // 2 * frame + (1 - q % 2) * frame // 2 :
                    q // 2 * frame + (2 - q % 2) * frame // 2
                ]
                for s in range(slabs)
                for q in range(2 * spec.frames)
            ]
        attended.append(jnp.concatenate(of_window, axis=0))
    for u in range(0, units, UNITS):
        total = jnp.zeros((step, slabs * tokens), jnp.float32)
        for h in range(heads):
            total = total + lax.dot_general(
                weight(h, u, UNITS, slice(3 * head, 4 * head)),
                attended[h],
                NT,
                preferred_element_type=jnp.float32,
            )
        total = total.astype(jnp.bfloat16)
        for slab in range(slabs):
            for k in range(UNITS):
                out_ref[slab, order[u + k]] = total[
                    k * rows : (k + 1) * rows, slab * tokens : (slab + 1) * tokens
                ]


class Spec:
    def __init__(self, frames, slab_rows, cols, total_rows):
        self.frames, self.slab_rows, self.half_cols = frames, slab_rows, cols // 2
        self.total_rows, self.total_cols = total_rows, cols


def row_offset(shifts):
    return jnp.where(shifts[1, 0] > WH // 2, shifts[1, 0] - WH, shifts[1, 0])


class First(Spec):
    block, heads, windows, slabs = 0, 1, 3, 2

    def first_rows(self, shifts):
        z = lax.axis_index("z8") * 2 + lax.axis_index("z2")
        first = 2 * self.slab_rows * z - row_offset(shifts) - self.slab_rows // 2
        return [first + self.total_rows + w * self.slab_rows for w in range(self.windows)]

    def unit(self, w, k):
        owner, odd = k >> 1, k & 1
        if w == 1:
            return odd * 48 + owner * 3 + 2
        return (w // 2) * 48 + owner * 3 + odd

    def order(self):
        odd, core = lax.axis_index("z2"), lax.axis_index("c")
        return [
            (2 * m + z) * 2 + x for x in (core, 1 - core) for z in (odd, 1 - odd) for m in range(8)
        ]


class Second(Spec):
    block, heads, windows, slabs = 1, 2, 1, 1

    def first_rows(self, shifts):
        slab = (lax.axis_index("z8") * 2 + lax.axis_index("z2")) * 2 + lax.axis_index("xh")
        return [self.slab_rows * slab - row_offset(shifts) + self.total_rows]

    def unit(self, w, k):
        return k

    def order(self):
        return list(range(32))


def run_block(spec, shifts, x, qk_gain, weights):
    rows, tokens = x.shape[1:]
    units = sum(w.size for w in weights) // (spec.heads * rows * 4 * qk_gain.shape[1])
    scratch = [pltpu.VMEM((spec.windows * tokens, units * rows), jnp.bfloat16)]
    if len(weights) == 1:
        scratch += [
            pltpu.VMEM(weights[0].shape, jnp.bfloat16),
            pltpu.SemaphoreType.DMA((spec.heads * CHUNKS,)),
        ]
    vmem = pl.BlockSpec(memory_space=pltpu.VMEM)
    smem = pl.BlockSpec(memory_space=pltpu.SMEM)
    return pl.pallas_call(
        functools.partial(block_kernel, spec, len(weights) == 1),
        out_shape=jax.ShapeDtypeStruct((spec.slabs, units, rows, tokens), jnp.bfloat16),
        in_specs=[smem, vmem, vmem]
        + [pl.BlockSpec(memory_space=pl.ANY) if len(weights) == 1 else vmem] * len(weights),
        out_specs=vmem,
        scratch_shapes=scratch,
        compiler_params=pltpu.CompilerParams(vmem_limit_bytes=40 * 1024 * 1024),
        cost_estimate=pl.CostEstimate(
            flops=2 * spec.windows * tokens * sum(w.size for w in weights),
            bytes_accessed=2 * sum(w.size for w in weights) + 4 * x.size,
            transcendentals=spec.heads * spec.windows * tokens * tokens,
        ),
        name="window_block",
    )(shifts, x, qk_gain, *weights)


def arrange_kernel(dims, copies, shifts, before_ref, own_ref, after_ref, pieces_ref, x_ref):
    frames, slab_rows, cols = dims
    count, local = own_ref.shape
    half, half_cols = count // 2, cols // 2
    x_hi = lax.axis_index("xh")
    tokens = jnp.concatenate([before_ref[...], own_ref[...], after_ref[...]], axis=0).T
    lane = lax.broadcasted_iota(jnp.int32, (1, count), 1)
    f = lax.bitwise_and(lax.div(lane, slab_rows * half_cols), frames - 1)
    r = lax.bitwise_and(lax.div(lane, half_cols), slab_rows - 1)
    j = lax.div(lane, half) * half_cols + lax.bitwise_and(lane, half_cols - 1)
    w = lax.bitwise_and(j - shifts[0, 1] + cols, cols - 1)

    def rows_from(start):
        row = start - row_offset(shifts) + r
        slab = lax.div(row, slab_rows)
        source = slab * count + f * (slab_rows * cols) + (row - slab * slab_rows) * cols + w
        hit = lax.broadcasted_iota(jnp.int32, (3 * count, count), 0) == source
        chosen = jnp.where(hit, 1.0, 0.0).astype(jnp.bfloat16)
        return jnp.dot(tokens, chosen, preferred_element_type=jnp.float32).astype(jnp.bfloat16)

    outer = rows_from(slab_rows // 2 + slab_rows * x_hi)
    middle = rows_from(slab_rows + slab_rows // 2 - slab_rows * x_hi)
    middle = jnp.where(x_hi == 0, middle[: local // 2], middle[local // 2 :])
    x_ref[...] = rows_from(slab_rows)
    for c in range(2):
        for i in range(copies):
            pieces_ref[2 * i + c, :local] = outer[:, c * half : (c + 1) * half]
            pieces_ref[2 * i + c, local:] = middle[:, c * half : (c + 1) * half]


def arrange(dims, copies, shifts, before, own, after):
    count, local = own.shape
    vmem = pl.BlockSpec(memory_space=pltpu.VMEM)
    return pl.pallas_call(
        functools.partial(arrange_kernel, dims, copies),
        out_shape=(
            jax.ShapeDtypeStruct((2 * copies, local + local // 2, count // 2), jnp.bfloat16),
            jax.ShapeDtypeStruct((local, count), jnp.bfloat16),
        ),
        in_specs=[pl.BlockSpec(memory_space=pltpu.SMEM)] + [vmem] * 3,
        out_specs=(vmem, vmem),
        compiler_params=pltpu.CompilerParams(vmem_limit_bytes=32 * 1024 * 1024),
        cost_estimate=pl.CostEstimate(
            flops=2 * local * 9 * count * count,
            bytes_accessed=2 * (copies + 4) * count * local,
            transcendentals=0,
        ),
        name="arrange_tokens",
    )(shifts, before, own, after)


def neighbour(x, distance):
    count = lax.axis_size(SP)
    return lax.ppermute(x, SP, [(i, (i - distance) % count) for i in range(count)])


def swap_cores(x):
    return lax.ppermute(x, "c", [(0, 1), (1, 0)])


def on_device(tokens, qkv_weight, out_weight, norm_gain, qk_gain, shifts):
    frames, slab_rows, cols, local = tokens.shape
    count = frames * slab_rows * cols
    half = count // 2
    half_cols = cols // 2
    tp_count = lax.axis_size(TP)
    head = qk_gain.shape[-1]
    shard_rows = out_weight.shape[-1]
    sp_count = lax.axis_size(SP)
    total_rows = slab_rows * sp_count
    sp_rank = lax.axis_index(SP)
    x_hi = lax.axis_index("xh")

    def shard(b):
        gain = lax.dynamic_slice_in_dim(norm_gain[b], sp_rank * shard_rows, shard_rows)
        scaled = qkv_weight[b].reshape(shard_rows, 3 * head).astype(jnp.float32) * gain[:, None]
        return jnp.concatenate([scaled.astype(jnp.bfloat16), out_weight[b].T], axis=1)

    turned = lax.ppermute(
        shard(0), ("xh", "c"), [(xh * 2 + c, c * 2 + xh) for xh in range(2) for c in range(2)]
    )
    mine = shard(1)
    theirs = lax.ppermute(mine, "xh", [(0, 1), (1, 0)])
    natural = tokens.reshape(count, local)
    slabs = [neighbour(natural, -1), natural, neighbour(natural, 1)]

    offset = row_offset(shifts)
    lane = jnp.arange(count, dtype=jnp.int32)
    nat_f, nat_r, nat_w = lane // (slab_rows * cols), lane // cols % slab_rows, lane % cols
    pos_f = lane // (slab_rows * half_cols) % frames
    pos_r = lane // half_cols % slab_rows
    pos_j = lane // half * half_cols + lane % half_cols

    def pick(rows_f, rows_r, rows_c, f, r, c):
        hit = (rows_f[:, None] == f[None]) & (rows_r[:, None] == r[None])
        return (hit & (rows_c[:, None] == c[None])).astype(jnp.bfloat16)

    def exact(terms, dims_):
        total = sum(
            lax.dot_general(a, b, dims_, preferred_element_type=jnp.float32) for a, b in terms
        )
        return total.astype(jnp.bfloat16)

    def spread(halves, copies):
        pieces = jnp.broadcast_to(jnp.stack(halves)[None], (copies, 2) + halves[0].shape)
        return pieces.reshape((copies * 2,) + halves[0].shape)

    def add_up(x_t, parts):
        parts = parts.reshape(-1, 2, local, half).astype(jnp.float32)
        total = jnp.sum(parts, axis=0)
        total = jnp.concatenate([total[0], total[1]], axis=1)
        return (x_t.astype(jnp.float32) + total).astype(jnp.bfloat16)

    pieces, x_t = arrange((frames, slab_rows, cols), tp_count, shifts, *slabs)
    pieces, turned = lax.optimization_barrier((pieces, turned))
    full = lax.all_to_all(pieces, ("xh",) + TP, 0, 0, tiled=True)
    near0 = lax.all_gather(turned, "z8", axis=0, tiled=True)
    near0, theirs, full = lax.optimization_barrier((near0, theirs, full))
    pair1 = jnp.where(
        x_hi == 0,
        jnp.concatenate([mine, theirs], axis=0),
        jnp.concatenate([theirs, mine], axis=0),
    )
    gathered1 = lax.all_gather(pair1, ("z8", "z2", "c"), axis=0, tiled=False)
    z_count = sp_count // 2
    far0 = lax.ppermute(
        near0,
        ("z8", "z2", "c"),
        [(z * 2 + c, (z + 1 - 2 * c) % z_count * 2 + c) for z in range(z_count) for c in range(2)],
    )
    sums = run_block(
        First(frames, slab_rows, cols, total_rows), shifts,
        full.reshape(-1, shard_rows, half), qk_gain[0],
        [near0, far0, swap_cores(near0), swap_cores(far0)],
    )
    parts = lax.all_to_all(
        sums.reshape(2 * tp_count, local, half), ("xh",) + TP, 0, 0, tiled=True
    )
    x_t = add_up(x_t, parts)

    old_j = (pos_j - shifts[1, 1] + shifts[0, 1]) % cols
    x_t = exact(
        [(x_t, pick(pos_f, pos_r, pos_j, pos_f, pos_r, old_j))], (((1,), (0,)), ((), ()))
    )
    full = lax.all_to_all(
        spread([x_t[:, :half], x_t[:, half:]], tp_count // 2), TP, 0, 0, tiled=True
    )
    sums = run_block(
        Second(frames, slab_rows, cols, total_rows), shifts,
        full.reshape(-1, shard_rows, half), qk_gain[1],
        [gathered1.reshape(z_count, 2, 2 * shard_rows, 4 * head)],
    )
    parts = lax.all_to_all(sums.reshape(tp_count, local, half), TP, 0, 0, tiled=True)
    x_t = add_up(x_t, parts)

    new_j = (nat_w + shifts[1, 1]) % cols
    moved = nat_r + offset
    result = exact(
        [
            (pick(nat_f, moved - slab_rows * s, new_j, pos_f, pos_r, pos_j), slab)
            for s, slab in ((0, x_t), (1, neighbour(x_t, 1)), (-1, neighbour(x_t, -1)))
        ],
        NT,
    )
    return result.reshape(frames, slab_rows, cols, local)


def solution(mesh):
    shape = mesh.devices.shape
    fine = Mesh(mesh.devices.reshape(shape[0] // 4, 2, 2, 2, shape[1] // 4, 2), SP + TP)
    placed = (
        P(None, SP, None, TP),
        P(None, SP, None, TP),
        P(None, TP, SP),
        P(),
        P(),
        P(),
    )
    return jax.shard_map(
        on_device, mesh=fine, in_specs=placed, out_specs=P(None, SP, None, TP), check_vma=False
    )
```

time: 204 us -> 202 us (level)
  blocking collectives: 34.2 us -> 44.3 us
  waiting for transfers between devices: 57.4 us -> 49.3 us
  other arithmetic: 7.16 us -> 4.7 us
    all_to_all x0 -> x1, blocking collectives: none -> 16 us  [on_device(): lax.all_to_all(spread([x_t[:, :half], x_t[:, half:]], tp_count // 2), TP,...]
    all_to_all x1 -> x0, waiting for transfers between devices: 11.2 us -> none  [on_device(): full = lax.all_to_all(spread(x_t, tp_count // 2), TP, 0, 0, tiled=True)]
    ppermute x4, starting transfers between devices: 18.2 us -> 24.8 us  [neighbour(): lax.ppermute(x, SP, [(i, (i - distance) % count) for i in range(count)])]
    all_to_all x1, waiting for transfers between devices: 5.92 us -> 0.01 us  [on_device(): full = lax.all_to_all(pieces, ('xh',) + TP, 0, 0, tiled=True)]
    all_gather x1, blocking collectives: 34.2 us -> 28.4 us  [on_device(): near0 = lax.all_gather(turned, 'z8', axis=0, tiled=True)]
    all_to_all x1 -> x0, starting transfers between devices: 5.23 us -> none  [on_device(): full = lax.all_to_all(spread(x_t, tp_count // 2), TP, 0, 0, tiled=True)]
    unnamed x8 -> x14, local copies, waits for them, and re-layouts: 1.9 us -> 6.91 us
    all_to_all x1, waiting for transfers between devices: 16.7 us -> 20.8 us  [on_device(): lax.all_to_all(sums.reshape(2 * tp_count, local, half), ('xh',) + TP, 0,...]
  transfers between devices with their start and end apart: 15 -> 13, of which waited for: 7 -> 7; matrix products, arithmetic and copies ran while one was open for 7% -> 4% of each run, Pallas kernels for 2% -> 2%
where the time goes in v3:
time: 202 us
  starting transfers between devices  65.7 us (33%)
  waiting for transfers between devices  49.3 us (24%)
  blocking collectives  44.3 us (22%)
  between operations  15.7 us (8%)
  local copies, waits for them, and re-layouts  10.4 us (5%)
  Pallas kernels  10.1 us (5%)
  other arithmetic  4.7 us (2%)
    all_gather x1, blocking collectives, on_device(): near0 = lax.all_gather(turned, 'z8', axis=0, tiled=True)  28.4 us
    ppermute x4, starting transfers between devices, neighbour(): lax.ppermute(x, SP, [(i, (i - distance) % count) for i in range(count)])  24.8 us
    all_to_all x1, waiting for transfers between devices, on_device(): lax.all_to_all(sums.reshape(2 * tp_count, local, half), ('xh',) + TP, 0,...  20.8 us
    all_to_all x1, blocking collectives, on_device(): lax.all_to_all(spread([x_t[:, :half], x_t[:, half:]], tp_count // 2), TP,...  16 us
    ppermute x2, starting transfers between devices, swap_cores(): return lax.ppermute(x, 'c', [(0, 1), (1, 0)])  14.1 us
    all_to_all x1, waiting for transfers between devices, on_device(): lax.all_to_all(sums.reshape(tp_count, local, half), TP, 0, 0, tiled=True)  10.4 us
    pallas_call x2, Pallas kernels, run_block(): pl.pallas_call(functools.partial(block_kernel, spec, len(weights) == 1),...  9 us
    unnamed x14, local copies, waits for them, and re-layouts  6.91 us
  transfers between devices with their start and end apart: 13, of which 7 were waited for; matrix products, arithmetic and copies ran while one was open for 4% of the time, Pallas kernels for 2%

profile of v3, /device:TPU:1, one launch (start us, length us, event | category | flops | bytes accessed | tf_op | source)
XLA Modules:
  0.0 201.5 jit_solution(3886052187967424905)
XLA Ops:
  6.5 5.5 %collective-permute-start = (bf16[256,192]{1,0:T(8,128)(2,1)}, bf16[256,192]{1,0:T(8,128)(2,1)S(1)}, u32[]{:S(2)}, u32[]{:S(2)}) collective-permute-start(bf16[256,192]{1,0:T(8,128)(2,1)} %bitcast.65), channel_id=1, source_target_pairs={{0,16},{16,32},{32,48},{48,64},{64,80},{80,96},{96,112},{112,128},... | collective-permute-start | bytes 294920 | tf_op jit(solution)/shard_map/ppermute | solution.py:276
  12.0 10.9 %collective-permute-start.1 = (bf16[256,192]{1,0:T(8,128)(2,1)}, bf16[256,192]{1,0:T(8,128)(2,1)S(1)}, u32[]{:S(2)}, u32[]{:S(2)}) collective-permute-start(bf16[256,192]{1,0:T(8,128)(2,1)} %bitcast.66), channel_id=1, source_target_pairs={{0,496},{16,0},{32,16},{48,32},{64,48},{80,64},{96,80},{112,96},{1... | collective-permute-start | bytes 294920 | tf_op jit(solution)/shard_map/ppermute | solution.py:276
  22.9 0.8 fusion.52
  23.7 0.9 slice_convert_fusion
  24.7 0.1 copy.12
  24.8 0.8 slice_bitcast_fusion.6
  25.6 0.1 dynamic-slice_bitcast_fusion
  25.6 0.1 fusion.13
  25.7 1.9 collective-permute-start.2
  27.7 0.0 collective-permute-done.before_ref
  27.7 0.0 collective-permute-done.1.after_ref
  27.7 0.0 copy-start.3
  27.7 0.7 copy-done.3
  28.4 0.9 copy-done.5
  29.3 1.1 arrange_tokens.1
  30.4 0.0 copy-start.2
  30.4 1.4 copy-done.2
  31.8 1.4 collective-permute-done.2
  33.2 6.3 %all-to-all-start = ((bf16[32,288,128]{2,1,0:T(8,128)(2,1)}), bf16[32,288,128]{2,1,0:T(8,128)(2,1)S(1)}, u32[]{:S(2)}, u32[]{:S(2)}) async-start(bf16[32,288,128]{2,1,0:T(8,128)(2,1)} %copy-done.2), calls=%async_computation | async-start | bytes 4718592 | tf_op jit(solution)/shard_map/all_to_all | solution.py:338
  39.5 0.0 copy-start.6
  39.5 0.0 copy-start.4
  39.5 0.0 all-gather.2.cloned.1.call-start
  39.6 0.1 copy.13
  39.7 0.1 fusion.12
  39.8 0.7 fusion.51
  40.4 4.8 %collective-permute-start.3 = (bf16[96,512]{1,0:T(8,128)(2,1)}, bf16[96,512]{1,0:T(8,128)(2,1)S(1)}, u32[]{:S(2)}, u32[]{:S(2)}) collective-permute-start(bf16[96,512]{1,0:T(8,128)(2,1)} %get-tuple-element.26), channel_id=1, source_target_pairs={{0,16},{16,0},{1,17},{17,1},{2,18},{18,2},{3,19},{19,3},{4,20},{20... | collective-permute-start | bytes 294920 | tf_op jit(solution)/shard_map/ppermute | solution.py:305
  45.2 28.4 %all_gather.7.refs_0_ = bf16[768,512]{1,0:T(8,128)(2,1)S(1)} all-gather(bf16[96,512]{1,0:T(8,128)(2,1)S(1)} %collective-permute-done.2), channel_id=1, replica_groups=mesh['z8'=8,'z2'=2,'xh'=2,'xl'=2,'y'=4,'c'=2] {'z8'}, dimensions={0}, use_global_device_ids=true | all-gather | bytes 884736 | tf_op jit(solution)/shard_map/all_gather | solution.py:339
  73.6 0.0 collective-permute-done.3
  73.6 0.0 all-to-all-done
  73.6 0.7 maximum_select_fusion
  74.3 0.0 all-gather.2.cloned.1.call-update
  74.3 3.3 %collective-permute-start.4 = (bf16[768,512]{1,0:T(8,128)(2,1)S(1)}, bf16[768,512]{1,0:T(8,128)(2,1)S(1)}, u32[]{:S(2)}, u32[]{:S(2)}) collective-permute-start(bf16[768,512]{1,0:T(8,128)(2,1)S(1)} %all_gather.7.refs_0_), channel_id=1, source_target_pairs={{0,32},{1,481},{32,64},{33,1},{64,96},{65,33},{96,128},{97,65},{12... | collective-permute-start | bytes 2359304 | tf_op jit(solution)/shard_map/ppermute | solution.py:348
  77.6 5.7 %collective-permute-start.5 = (bf16[768,512]{1,0:T(8,128)(2,1)S(1)}, bf16[768,512]{1,0:T(8,128)(2,1)S(1)}, u32[]{:S(2)}, u32[]{:S(2)}) collective-permute-start(bf16[768,512]{1,0:T(8,128)(2,1)S(1)} %all_gather.7.refs_0_), channel_id=1, source_target_pairs={{0,1},{1,0},{2,3},{3,2},{4,5},{5,4},{6,7},{7,6},{8,9},{9,8},{10,11... | collective-permute-start | bytes 2359304 | tf_op jit(solution)/shard_map/ppermute | solution.py:280
  83.3 4.8 %collective-permute-done.4.refs_1_ = bf16[768,512]{1,0:T(8,128)(2,1)S(1)} collective-permute-done((bf16[768,512]{1,0:T(8,128)(2,1)S(1)}, bf16[768,512]{1,0:T(8,128)(2,1)S(1)}, u32[]{:S(2)}, u32[]{:S(2)}) %collective-permute-start.4) | collective-permute-done | bytes 786464 | tf_op jit(solution)/shard_map/ppermute | solution.py:348
  88.1 8.4 %collective-permute-start.6 = (bf16[768,512]{1,0:T(8,128)(2,1)S(1)}, bf16[768,512]{1,0:T(8,128)(2,1)S(1)}, u32[]{:S(2)}, u32[]{:S(2)}) collective-permute-start(bf16[768,512]{1,0:T(8,128)(2,1)S(1)} %collective-permute-done.4.refs_1_), channel_id=1, source_target_pairs={{0,1},{1,0},{2,3},{3,2},{4,5},{5,4},{6,7},{7,6},{8,9},{9,8},{10,11... | collective-permute-start | bytes 2359304 | tf_op jit(solution)/shard_map/ppermute | solution.py:280
  96.5 0.0 copy-done.6
  96.5 0.0 collective-permute-done.5.refs_2_
  96.5 1.9 collective-permute-done.6.refs_3_
  98.4 3.4 %window_block.2 = bf16[2,32,96,128]{3,2,1,0:T(8,128)(2,1)S(1)} custom-call(s32[2,2]{1,0:T(2,128)S(1)} %copy-done.4, bf16[96,96,128]{2,1,0:T(8,128)(2,1)S(1)} %bitcast.61, f32[2,128]{1,0:T(2,128)S(1)} %get-tuple-element.34.qk_gain_ref, bf16[768,512]{1,0:T(8,128)(2,1)S(1)} %all_gather.7.refs_0_, bf16[768,512]{1,0:T(8,128)(2,1)S(1)} %collective-permute-done.4.refs_1_, ...), custom_call_target="tpu_custom_call" | custom-call | flops 1207959552 | bytes 7864320 | tf_op jit(solution)/shard_map/window_block/pallas_call | solution.py:206
  101.8 0.0 copy-start.1
  101.8 1.1 copy-done.1
  102.9 5.1 %all-to-all-start.1 = ((bf16[32,192,128]{2,1,0:T(8,128)(2,1)}), bf16[32,192,128]{2,1,0:T(8,128)(2,1)S(1)}, u32[]{:S(2)}, u32[]{:S(2)}) async-start(bf16[32,192,128]{2,1,0:T(8,128)(2,1)} %bitcast.63), calls=%async_computation.1 | async-start | bytes 3145728 | tf_op jit(solution)/shard_map/all_to_all | solution.py:358
  108.0 0.6 fusion.53
  108.7 1.2 and_select_fusion
  109.9 20.8 %all-to-all-done.1 = bf16[32,192,128]{2,1,0:T(8,128)(2,1)S(1)} async-done(((bf16[32,192,128]{2,1,0:T(8,128)(2,1)}), bf16[32,192,128]{2,1,0:T(8,128)(2,1)S(1)}, u32[]{:S(2)}, u32[]{:S(2)}) %all-to-all-start.1) | async-done | bytes 1572896 | tf_op jit(solution)/shard_map/all_to_all | solution.py:358
  130.7 0.2 convert_reduce_fusion
  131.0 0.3 convolution_convert_fusion
  131.3 0.1 broadcast_in_dim.2
  131.5 16.0 %all_to_all.20 = bf16[16,192,128]{2,1,0:T(8,128)(2,1)S(1)} all-to-all(bf16[16,192,128]{2,1,0:T(8,128)(2,1)S(1)} %bitcast.69), channel_id=1, replica_groups=mesh['z8'=8,'z2'=2,'xh'=2,'xl'=2,'y'=4,'c'=2] {'xl','y','c'}, dimensions={0} | all-to-all | bytes 1572864 | tf_op jit(solution)/shard_map/all_to_all | solution.py:367
  147.4 3.6 %all-gather.2.cloned.1.call-done = bf16[32,192,512]{2,1,0:T(8,128)(2,1)} async-done(((bf16[1,192,512]{2,1,0:T(8,128)(2,1)}), bf16[32,192,512]{2,1,0:T(8,128)(2,1)}) %all-gather.2.cloned.1.call-update) | async-done | bytes 6291472 | tf_op jit(solution)/shard_map/all_gather | solution.py:346
  151.1 2.8 %copy-done = bf16[32,192,512]{2,1,0:T(8,128)(2,1)S(1)} copy-done((bf16[32,192,512]{2,1,0:T(8,128)(2,1)S(1)}, bf16[32,192,512]{2,1,0:T(8,128)(2,1)}, u32[]{:S(2)}) %copy-start) | copy-done | bytes 6291480
  153.8 5.6 %window_block.3 = bf16[1,32,96,128]{3,2,1,0:T(8,128)(2,1)} custom-call(s32[2,2]{1,0:T(2,128)S(1)} %copy-done.4, bf16[32,96,128]{2,1,0:T(8,128)(2,1)S(1)} %bitcast.64, f32[2,128]{1,0:T(2,128)S(1)} %get-tuple-element.33.qk_gain_ref, bf16[16,2,192,512]{3,2,1,0:T(8,128)(2,1)S(1)} %bitcast.62), custom_call_target="tpu_custom_call" | custom-call | flops 805306368 | bytes 7864320 | tf_op jit(solution)/shard_map/window_block/pallas_call | solution.py:206
  159.5 5.4 %all-to-all-start.3 = ((bf16[16,192,128]{2,1,0:T(8,128)(2,1)}), bf16[16,192,128]{2,1,0:T(8,128)(2,1)S(1)}, u32[]{:S(2)}, u32[]{:S(2)}) async-start(bf16[16,192,128]{2,1,0:T(8,128)(2,1)} %bitcast.24), calls=%async_computation.3 | async-start | bytes 1572864 | tf_op jit(solution)/shard_map/all_to_all | solution.py:375
  166.9 0.6 and_select_fusion.2
  167.5 10.4 %all-to-all-done.3 = bf16[16,192,128]{2,1,0:T(8,128)(2,1)S(1)} async-done(((bf16[16,192,128]{2,1,0:T(8,128)(2,1)}), bf16[16,192,128]{2,1,0:T(8,128)(2,1)S(1)}, u32[]{:S(2)}, u32[]{:S(2)}) %all-to-all-start.3) | async-done | bytes 786464 | tf_op jit(solution)/shard_map/all_to_all | solution.py:375
  177.9 0.1 convert_reduce_fusion.1
  178.1 6.6 %collective-permute-start.7 = (bf16[192,256]{1,0:T(8,128)(2,1)S(1)}, bf16[192,256]{1,0:T(8,128)(2,1)S(1)}, u32[]{:S(2)}, u32[]{:S(2)}) collective-permute-start(bf16[192,256]{1,0:T(8,128)(2,1)S(1)} %fusion.11), channel_id=1, source_target_pairs={{0,496},{16,0},{32,16},{48,32},{64,48},{80,64},{96,80},{112,96},{1... | collective-permute-start | bytes 294920 | tf_op jit(solution)/shard_map/ppermute | solution.py:276
  184.6 1.9 collective-permute-start.8
  186.6 0.3 fusion.1
  186.9 0.0 collective-permute-done.7
  186.9 0.3 convolution_add_fusion.1
  187.2 6.4 %collective-permute-done.8 = bf16[192,256]{1,0:T(8,128)(2,1)S(1)} collective-permute-done((bf16[192,256]{1,0:T(8,128)(2,1)S(1)}, bf16[192,256]{1,0:T(8,128)(2,1)S(1)}, u32[]{:S(2)}, u32[]{:S(2)}) %collective-permute-start.8) | collective-permute-done | bytes 98336 | tf_op jit(solution)/shard_map/ppermute | solution.py:276
  193.6 0.3 fusion
  193.9 0.8 copy.14
  (14 shorter events, 0.1 us)
Async XLA Ops:
  6.5 21.1 %collective-permute-start = (bf16[256,192]{1,0:T(8,128)(2,1)}, bf16[256,192]{1,0:T(8,128)(2,1)S(1)}, u32[]{:S(2)}, u32[]{:S(2)}) collective-permute-start(bf16[256,192]{1,0:T(8,128)(2,1)} %bitcast.65), channel_id=1, source_target_pairs={{0,16},{16,32},{32,48},{48,64},{64,80},{80,96},{96,112},{112,128},... | collective-permute-start | bytes 294920 | tf_op jit(solution)/shard_map/ppermute | solution.py:276
  12.0 15.7 %collective-permute-start.1 = (bf16[256,192]{1,0:T(8,128)(2,1)}, bf16[256,192]{1,0:T(8,128)(2,1)S(1)}, u32[]{:S(2)}, u32[]{:S(2)}) collective-permute-start(bf16[256,192]{1,0:T(8,128)(2,1)} %bitcast.66), channel_id=1, source_target_pairs={{0,496},{16,0},{32,16},{48,32},{64,48},{80,64},{96,80},{112,96},{1... | collective-permute-start | bytes 294920 | tf_op jit(solution)/shard_map/ppermute | solution.py:276
  25.7 7.4 %collective-permute-start.2 = (bf16[96,512]{1,0:T(8,128)(2,1)S(1)}, bf16[96,512]{1,0:T(8,128)(2,1)S(1)}, u32[]{:S(2)}, u32[]{:S(2)}) collective-permute-start(bf16[96,512]{1,0:T(8,128)(2,1)S(1)} %pad_maximum_fusion), channel_id=1, source_target_pairs={{0,0},{1,16},{16,1},{17,17},{2,2},{3,18},{18,3},{19,19},{4,4},{5,2... | collective-permute-start | bytes 294920 | tf_op jit(solution)/shard_map/ppermute | solution.py:301
  27.7 0.7 copy-start.3
  28.4 0.9 copy-start.5
  30.4 1.4 copy-start.2
  33.2 40.4 %all-to-all-start = ((bf16[32,288,128]{2,1,0:T(8,128)(2,1)}), bf16[32,288,128]{2,1,0:T(8,128)(2,1)S(1)}, u32[]{:S(2)}, u32[]{:S(2)}) async-start(bf16[32,288,128]{2,1,0:T(8,128)(2,1)} %copy-done.2), calls=%async_computation | async-start | bytes 4718592 | tf_op jit(solution)/shard_map/all_to_all | solution.py:338
  39.5 57.0 %copy-start.6 = (f32[2,2,128]{2,1,0:T(2,128)S(1)}, f32[2,2,128]{2,1,0:T(2,128)}, u32[]{:S(2)}) copy-start(f32[2,2,128]{2,1,0:T(2,128)} %param.10) | copy-start | bytes 6148
  39.5 58.9 %copy-start.4 = (s32[2,2]{1,0:T(2,128)S(1)}, s32[2,2]{1,0:T(2,128)}, u32[]{:S(2)}) copy-start(s32[2,2]{1,0:T(2,128)} %shifts.5) | copy-start | bytes 52
  39.5 111.5 %all-gather.2.cloned.1.call-start = ((), (), s32[]{:S(2)}) async-start(), calls=%async_computation.4 | async-start | bytes 6488064 | tf_op jit(solution)/shard_map/all_gather | solution.py:346
  40.4 33.2 %collective-permute-start.3 = (bf16[96,512]{1,0:T(8,128)(2,1)}, bf16[96,512]{1,0:T(8,128)(2,1)S(1)}, u32[]{:S(2)}, u32[]{:S(2)}) collective-permute-start(bf16[96,512]{1,0:T(8,128)(2,1)} %get-tuple-element.26), channel_id=1, source_target_pairs={{0,16},{16,0},{1,17},{17,1},{2,18},{18,2},{3,19},{19,3},{4,20},{20... | collective-permute-start | bytes 294920 | tf_op jit(solution)/shard_map/ppermute | solution.py:305
  74.3 13.8 %collective-permute-start.4 = (bf16[768,512]{1,0:T(8,128)(2,1)S(1)}, bf16[768,512]{1,0:T(8,128)(2,1)S(1)}, u32[]{:S(2)}, u32[]{:S(2)}) collective-permute-start(bf16[768,512]{1,0:T(8,128)(2,1)S(1)} %all_gather.7.refs_0_), channel_id=1, source_target_pairs={{0,32},{1,481},{32,64},{33,1},{64,96},{65,33},{96,128},{97,65},{12... | collective-permute-start | bytes 2359304 | tf_op jit(solution)/shard_map/ppermute | solution.py:348
  77.6 18.9 %collective-permute-start.5 = (bf16[768,512]{1,0:T(8,128)(2,1)S(1)}, bf16[768,512]{1,0:T(8,128)(2,1)S(1)}, u32[]{:S(2)}, u32[]{:S(2)}) collective-permute-start(bf16[768,512]{1,0:T(8,128)(2,1)S(1)} %all_gather.7.refs_0_), channel_id=1, source_target_pairs={{0,1},{1,0},{2,3},{3,2},{4,5},{5,4},{6,7},{7,6},{8,9},{9,8},{10,11... | collective-permute-start | bytes 2359304 | tf_op jit(solution)/shard_map/ppermute | solution.py:280
  88.1 10.3 %collective-permute-start.6 = (bf16[768,512]{1,0:T(8,128)(2,1)S(1)}, bf16[768,512]{1,0:T(8,128)(2,1)S(1)}, u32[]{:S(2)}, u32[]{:S(2)}) collective-permute-start(bf16[768,512]{1,0:T(8,128)(2,1)S(1)} %collective-permute-done.4.refs_1_), channel_id=1, source_target_pairs={{0,1},{1,0},{2,3},{3,2},{4,5},{5,4},{6,7},{7,6},{8,9},{9,8},{10,11... | collective-permute-start | bytes 2359304 | tf_op jit(solution)/shard_map/ppermute | solution.py:280
  101.8 1.1 copy-start.1
  102.9 27.8 %all-to-all-start.1 = ((bf16[32,192,128]{2,1,0:T(8,128)(2,1)}), bf16[32,192,128]{2,1,0:T(8,128)(2,1)S(1)}, u32[]{:S(2)}, u32[]{:S(2)}) async-start(bf16[32,192,128]{2,1,0:T(8,128)(2,1)} %bitcast.63), calls=%async_computation.1 | async-start | bytes 3145728 | tf_op jit(solution)/shard_map/all_to_all | solution.py:358
  151.1 2.8 %copy-start = (bf16[32,192,512]{2,1,0:T(8,128)(2,1)S(1)}, bf16[32,192,512]{2,1,0:T(8,128)(2,1)}, u32[]{:S(2)}) copy-start(bf16[32,192,512]{2,1,0:T(8,128)(2,1)} %all-gather.2.cloned.1.call-done) | copy-start | bytes 18874372
  159.5 18.4 %all-to-all-start.3 = ((bf16[16,192,128]{2,1,0:T(8,128)(2,1)}), bf16[16,192,128]{2,1,0:T(8,128)(2,1)S(1)}, u32[]{:S(2)}, u32[]{:S(2)}) async-start(bf16[16,192,128]{2,1,0:T(8,128)(2,1)} %bitcast.24), calls=%async_computation.3 | async-start | bytes 1572864 | tf_op jit(solution)/shard_map/all_to_all | solution.py:375
  178.1 8.8 %collective-permute-start.7 = (bf16[192,256]{1,0:T(8,128)(2,1)S(1)}, bf16[192,256]{1,0:T(8,128)(2,1)S(1)}, u32[]{:S(2)}, u32[]{:S(2)}) collective-permute-start(bf16[192,256]{1,0:T(8,128)(2,1)S(1)} %fusion.11), channel_id=1, source_target_pairs={{0,496},{16,0},{32,16},{48,32},{64,48},{80,64},{96,80},{112,96},{1... | collective-permute-start | bytes 294920 | tf_op jit(solution)/shard_map/ppermute | solution.py:276
  184.6 9.0 %collective-permute-start.8 = (bf16[192,256]{1,0:T(8,128)(2,1)S(1)}, bf16[192,256]{1,0:T(8,128)(2,1)S(1)}, u32[]{:S(2)}, u32[]{:S(2)}) collective-permute-start(bf16[192,256]{1,0:T(8,128)(2,1)S(1)} %fusion.11), channel_id=1, source_target_pairs={{0,16},{16,32},{32,48},{48,64},{64,80},{80,96},{96,112},{112,128},... | collective-permute-start | bytes 294920 | tf_op jit(solution)/shard_map/ppermute | solution.py:276
Sparse Core Ops, SparseCore 0:
  74.4 76.5 all-gather.1

commit v4 on v3

--- a/solution.py
+++ b/solution.py
@@ -11,7 +11,7 @@
 WH = 4
 WW = 8
 UNITS = 4
-CHUNKS = 4
+CHUNKS = 8
 TP = ("xl", "y", "c")
 SP = ("z8", "z2", "xh")
 NT = (((1,), (1,)), ((), ()))
@@ -42,15 +42,12 @@
         source, out_ref, x_rows_ref, held_ref, sems = refs
         weights = [held_ref]
         size = source.shape[0] // CHUNKS
-        for h in range(source.shape[1]):
-            for n in range(CHUNKS):
-                there = slice(n * size, (n + 1) * size)
-                copies.append(
-                    pltpu.make_async_copy(
-                        source.at[there, h], held_ref.at[there, h], sems.at[h * CHUNKS + n]
-                    )
-                )
-                copies[-1].start()
+        for n in range(CHUNKS):
+            there = slice(n * size, (n + 1) * size)
+            copies.append(
+                pltpu.make_async_copy(source.at[there], held_ref.at[there], sems.at[n])
+            )
+            copies[-1].start()
     else:
         weights, (out_ref, x_rows_ref) = refs[:-2], refs[-2:]
     slabs, units, rows, tokens = out_ref.shape
@@ -97,23 +94,24 @@
             )
             x_rows_ref[w * tokens : (w + 1) * tokens, u * rows : u * rows + step] = block.T
 
-    attended = []
-    for h in range(heads):
-        projected = jnp.zeros((windows * tokens, 3 * head), jnp.float32)
-        for u in range(0, units, part):
-            if copies:
-                copies[h * CHUNKS + u // part].wait()
-            projected = projected + jnp.dot(
+    projected = [jnp.zeros((windows * tokens, 3 * head), jnp.float32)] * heads
+    for u in range(0, units, part):
+        if copies:
+            copies[u // part].wait()
+        for h in range(heads):
+            projected[h] = projected[h] + jnp.dot(
                 x_rows_ref[:, u * rows : (u + part) * rows],
                 weight(h, u, part, slice(0, 3 * head)),
                 preferred_element_type=jnp.float32,
             )
+    attended = []
+    for h in range(heads):
         of_window = []
         for w in range(windows):
             first_row = first_rows[w]
             of_window.append(
                 head_attention(
-                    projected[w * tokens : (w + 1) * tokens],
+                    projected[h][w * tokens : (w + 1) * tokens],
                     scales[w],
                     qk_gain_ref[...],
                     window(first_row, 0) == window(first_row, 1),
@@ -199,7 +197,7 @@
     if len(weights) == 1:
         scratch += [
             pltpu.VMEM(weights[0].shape, jnp.bfloat16),
-            pltpu.SemaphoreType.DMA((spec.heads * CHUNKS,)),
+            pltpu.SemaphoreType.DMA((CHUNKS,)),
         ]
     vmem = pl.BlockSpec(memory_space=pltpu.VMEM)
     smem = pl.BlockSpec(memory_space=pltpu.SMEM)
@@ -210,7 +208,9 @@
         + [pl.BlockSpec(memory_space=pl.ANY) if len(weights) == 1 else vmem] * len(weights),
         out_specs=vmem,
         scratch_shapes=scratch,
-        compiler_params=pltpu.CompilerParams(vmem_limit_bytes=40 * 1024 * 1024),
+        compiler_params=pltpu.CompilerParams(
+            vmem_limit_bytes=(58 if len(weights) == 1 else 40) * 1024 * 1024
+        ),
         cost_estimate=pl.CostEstimate(
             flops=2 * spec.windows * tokens * sum(w.size for w in weights),
             bytes_accessed=2 * sum(w.size for w in weights) + 4 * x.size,

time: 202 us -> 200 us (0.990)
  local copies, waits for them, and re-layouts: 10.4 us -> 8.18 us
    unnamed x14 -> x12, local copies, waits for them, and re-layouts: 6.91 us -> 4.14 us
where the time goes in v4:
time: 200 us; the launch traced here: 199 us
  starting transfers between devices  65.7 us (33%)
  waiting for transfers between devices  47.4 us (24%)
  blocking collectives  45.1 us (23%)
  between operations  15.8 us (8%)
  Pallas kernels  11.2 us (6%)
  local copies, waits for them, and re-layouts  8.18 us (4%)
  other arithmetic  4.72 us (2%)
    all_gather x1, blocking collectives, on_device(): near0 = lax.all_gather(turned, 'z8', axis=0, tiled=True)  28.4 us
    ppermute x4, starting transfers between devices, neighbour(): lax.ppermute(x, SP, [(i, (i - distance) % count) for i in range(count)])  25 us
    all_to_all x1, waiting for transfers between devices, on_device(): lax.all_to_all(sums.reshape(2 * tp_count, local, half), ('xh',) + TP, 0,...  20.8 us
    all_to_all x1, blocking collectives, on_device(): lax.all_to_all(spread([x_t[:, :half], x_t[:, half:]], tp_count // 2), TP,...  16.6 us
    ppermute x2, starting transfers between devices, swap_cores(): return lax.ppermute(x, 'c', [(0, 1), (1, 0)])  14.2 us
    all_to_all x1, waiting for transfers between devices, on_device(): lax.all_to_all(sums.reshape(tp_count, local, half), TP, 0, 0, tiled=True)  10.3 us
    pallas_call x2, Pallas kernels, run_block(): pl.pallas_call(functools.partial(block_kernel, spec, len(weights) == 1),...  10.1 us
    ppermute x4, waiting for transfers between devices, neighbour(): lax.ppermute(x, SP, [(i, (i - distance) % count) for i in range(count)])  6.4 us
  transfers between devices with their start and end apart: 13, of which 7 were waited for; matrix products, arithmetic and copies ran while one was open for 4% of the time, Pallas kernels for 2%

profile of v4, /device:TPU:1, one launch (start us, length us, event | category | flops | bytes accessed | tf_op | source)
XLA Modules:
  0.0 199.3 jit_solution(15731268407100502960)
XLA Ops:
  6.5 5.5 %collective-permute-start = (bf16[256,192]{1,0:T(8,128)(2,1)}, bf16[256,192]{1,0:T(8,128)(2,1)S(1)}, u32[]{:S(2)}, u32[]{:S(2)}) collective-permute-start(bf16[256,192]{1,0:T(8,128)(2,1)} %bitcast.63), channel_id=1, source_target_pairs={{0,16},{16,32},{32,48},{48,64},{64,80},{80,96},{96,112},{112,128},... | collective-permute-start | bytes 294920 | tf_op jit(solution)/shard_map/ppermute | solution.py:276
  12.0 10.9 %collective-permute-start.1 = (bf16[256,192]{1,0:T(8,128)(2,1)}, bf16[256,192]{1,0:T(8,128)(2,1)S(1)}, u32[]{:S(2)}, u32[]{:S(2)}) collective-permute-start(bf16[256,192]{1,0:T(8,128)(2,1)} %bitcast.64), channel_id=1, source_target_pairs={{0,496},{16,0},{32,16},{48,32},{64,48},{80,64},{96,80},{112,96},{1... | collective-permute-start | bytes 294920 | tf_op jit(solution)/shard_map/ppermute | solution.py:276
  22.9 0.8 fusion.52
  23.7 0.9 slice_convert_fusion
  24.7 0.1 copy.12
  24.8 0.8 slice_bitcast_fusion.6
  25.6 0.1 dynamic-slice_bitcast_fusion
  25.6 0.1 fusion.13
  25.7 1.9 collective-permute-start.2
  27.7 0.0 collective-permute-done.before_ref
  27.7 0.0 collective-permute-done.1.after_ref
  27.7 0.0 copy-start.2
  27.7 0.7 copy-done.2
  28.4 0.9 copy-done.4
  29.3 1.1 arrange_tokens.1
  30.4 0.0 copy-start.1
  30.4 1.4 copy-done.1
  31.8 1.4 collective-permute-done.2
  33.2 6.3 %all-to-all-start = ((bf16[32,288,128]{2,1,0:T(8,128)(2,1)}), bf16[32,288,128]{2,1,0:T(8,128)(2,1)S(1)}, u32[]{:S(2)}, u32[]{:S(2)}) async-start(bf16[32,288,128]{2,1,0:T(8,128)(2,1)} %copy-done.1), calls=%async_computation | async-start | bytes 4718592 | tf_op jit(solution)/shard_map/all_to_all | solution.py:338
  39.5 0.0 copy-start.5
  39.5 0.0 copy-start.3
  39.5 0.0 all-gather.2.cloned.1.call-start
  39.6 0.1 copy.13
  39.7 0.1 fusion.12
  39.8 0.7 fusion.51
  40.4 4.8 %collective-permute-start.3 = (bf16[96,512]{1,0:T(8,128)(2,1)}, bf16[96,512]{1,0:T(8,128)(2,1)S(1)}, u32[]{:S(2)}, u32[]{:S(2)}) collective-permute-start(bf16[96,512]{1,0:T(8,128)(2,1)} %get-tuple-element.26), channel_id=1, source_target_pairs={{0,16},{16,0},{1,17},{17,1},{2,18},{18,2},{3,19},{19,3},{4,20},{20... | collective-permute-start | bytes 294920 | tf_op jit(solution)/shard_map/ppermute | solution.py:305
  45.2 28.4 %all_gather.7.refs_0_ = bf16[768,512]{1,0:T(8,128)(2,1)S(1)} all-gather(bf16[96,512]{1,0:T(8,128)(2,1)S(1)} %collective-permute-done.2), channel_id=1, replica_groups=mesh['z8'=8,'z2'=2,'xh'=2,'xl'=2,'y'=4,'c'=2] {'z8'}, dimensions={0}, use_global_device_ids=true | all-gather | bytes 884736 | tf_op jit(solution)/shard_map/all_gather | solution.py:339
  73.6 0.0 collective-permute-done.3
  73.6 0.0 all-to-all-done
  73.7 0.7 maximum_select_fusion
  74.4 0.0 all-gather.2.cloned.1.call-update
  74.4 3.3 %collective-permute-start.4 = (bf16[768,512]{1,0:T(8,128)(2,1)S(1)}, bf16[768,512]{1,0:T(8,128)(2,1)S(1)}, u32[]{:S(2)}, u32[]{:S(2)}) collective-permute-start(bf16[768,512]{1,0:T(8,128)(2,1)S(1)} %all_gather.7.refs_0_), channel_id=1, source_target_pairs={{0,32},{1,481},{32,64},{33,1},{64,96},{65,33},{96,128},{97,65},{12... | collective-permute-start | bytes 2359304 | tf_op jit(solution)/shard_map/ppermute | solution.py:348
  77.7 5.7 %collective-permute-start.5 = (bf16[768,512]{1,0:T(8,128)(2,1)S(1)}, bf16[768,512]{1,0:T(8,128)(2,1)S(1)}, u32[]{:S(2)}, u32[]{:S(2)}) collective-permute-start(bf16[768,512]{1,0:T(8,128)(2,1)S(1)} %all_gather.7.refs_0_), channel_id=1, source_target_pairs={{0,1},{1,0},{2,3},{3,2},{4,5},{5,4},{6,7},{7,6},{8,9},{9,8},{10,11... | collective-permute-start | bytes 2359304 | tf_op jit(solution)/shard_map/ppermute | solution.py:280
  83.3 4.6 %collective-permute-done.4.refs_1_ = bf16[768,512]{1,0:T(8,128)(2,1)S(1)} collective-permute-done((bf16[768,512]{1,0:T(8,128)(2,1)S(1)}, bf16[768,512]{1,0:T(8,128)(2,1)S(1)}, u32[]{:S(2)}, u32[]{:S(2)}) %collective-permute-start.4) | collective-permute-done | bytes 786464 | tf_op jit(solution)/shard_map/ppermute | solution.py:348
  88.0 8.6 %collective-permute-start.6 = (bf16[768,512]{1,0:T(8,128)(2,1)S(1)}, bf16[768,512]{1,0:T(8,128)(2,1)S(1)}, u32[]{:S(2)}, u32[]{:S(2)}) collective-permute-start(bf16[768,512]{1,0:T(8,128)(2,1)S(1)} %collective-permute-done.4.refs_1_), channel_id=1, source_target_pairs={{0,1},{1,0},{2,3},{3,2},{4,5},{5,4},{6,7},{7,6},{8,9},{9,8},{10,11... | collective-permute-start | bytes 2359304 | tf_op jit(solution)/shard_map/ppermute | solution.py:280
  96.6 0.0 copy-done.5
  96.6 0.6 slice_bitcast_fusion.8
  97.1 0.0 collective-permute-done.5.refs_2_
  97.2 1.4 collective-permute-done.6.refs_3_
  98.5 0.0 copy-done.3
  98.5 3.4 %window_block.2 = bf16[2,32,96,128]{3,2,1,0:T(8,128)(2,1)S(1)} custom-call(s32[2,2]{1,0:T(2,128)S(1)} %copy-done.3, bf16[96,96,128]{2,1,0:T(8,128)(2,1)S(1)} %bitcast.61, f32[2,128]{1,0:T(2,128)S(1)} %get-tuple-element.34.qk_gain_ref, bf16[768,512]{1,0:T(8,128)(2,1)S(1)} %all_gather.7.refs_0_, bf16[768,512]{1,0:T(8,128)(2,1)S(1)} %collective-permute-done.4.refs_1_, ...), custom_call_target="tpu_custom_call" | custom-call | flops 1207959552 | bytes 7864320 | tf_op jit(solution)/shard_map/window_block/pallas_call | solution.py:204
  101.9 1.1 copy-done
  103.1 4.9 %all-to-all-start.1 = ((bf16[32,192,128]{2,1,0:T(8,128)(2,1)}), bf16[32,192,128]{2,1,0:T(8,128)(2,1)S(1)}, u32[]{:S(2)}, u32[]{:S(2)}) async-start(bf16[32,192,128]{2,1,0:T(8,128)(2,1)} %bitcast.62), calls=%async_computation.1 | async-start | bytes 3145728 | tf_op jit(solution)/shard_map/all_to_all | solution.py:358
  108.0 0.6 fusion.53
  108.7 1.2 and_select_fusion
  109.9 20.8 %all-to-all-done.1 = bf16[32,192,128]{2,1,0:T(8,128)(2,1)S(1)} async-done(((bf16[32,192,128]{2,1,0:T(8,128)(2,1)}), bf16[32,192,128]{2,1,0:T(8,128)(2,1)S(1)}, u32[]{:S(2)}, u32[]{:S(2)}) %all-to-all-start.1) | async-done | bytes 1572896 | tf_op jit(solution)/shard_map/all_to_all | solution.py:358
  130.7 0.2 convert_reduce_fusion
  130.9 0.3 convolution_convert_fusion
  131.3 0.1 broadcast_in_dim.2
  131.4 16.6 %all_to_all.20 = bf16[16,192,128]{2,1,0:T(8,128)(2,1)} all-to-all(bf16[16,192,128]{2,1,0:T(8,128)(2,1)S(1)} %bitcast.70), channel_id=1, replica_groups=mesh['z8'=8,'z2'=2,'xh'=2,'xl'=2,'y'=4,'c'=2] {'xl','y','c'}, dimensions={0} | all-to-all | bytes 1572864 | tf_op jit(solution)/shard_map/all_to_all | solution.py:367
  148.1 2.4 %all-gather.2.cloned.1.call-done = bf16[32,192,512]{2,1,0:T(8,128)(2,1)} async-done(((bf16[1,192,512]{2,1,0:T(8,128)(2,1)}), bf16[32,192,512]{2,1,0:T(8,128)(2,1)}) %all-gather.2.cloned.1.call-update) | async-done | bytes 6291472 | tf_op jit(solution)/shard_map/all_gather | solution.py:346
  150.5 6.7 %window_block.3 = bf16[1,32,96,128]{3,2,1,0:T(8,128)(2,1)} custom-call(s32[2,2]{1,0:T(2,128)} %shifts.5, bf16[32,96,128]{2,1,0:T(8,128)(2,1)} %bitcast.69, f32[2,128]{1,0:T(2,128)} %get-tuple-element.33.qk_gain_ref, bf16[16,2,192,512]{3,2,1,0:T(8,128)(2,1)} %bitcast.67), custom_call_target="tpu_custom_call" | custom-call | flops 805306368 | bytes 7864320 | tf_op jit(solution)/shard_map/window_block/pallas_call | solution.py:204
  157.2 5.3 %all-to-all-start.3 = ((bf16[16,192,128]{2,1,0:T(8,128)(2,1)}), bf16[16,192,128]{2,1,0:T(8,128)(2,1)S(1)}, u32[]{:S(2)}, u32[]{:S(2)}) async-start(bf16[16,192,128]{2,1,0:T(8,128)(2,1)} %bitcast.68), calls=%async_computation.3 | async-start | bytes 1572864 | tf_op jit(solution)/shard_map/all_to_all | solution.py:375
  164.6 0.6 and_select_fusion.2
  165.2 10.3 %all-to-all-done.3 = bf16[16,192,128]{2,1,0:T(8,128)(2,1)S(1)} async-done(((bf16[16,192,128]{2,1,0:T(8,128)(2,1)}), bf16[16,192,128]{2,1,0:T(8,128)(2,1)S(1)}, u32[]{:S(2)}, u32[]{:S(2)}) %all-to-all-start.3) | async-done | bytes 786464 | tf_op jit(solution)/shard_map/all_to_all | solution.py:375
  175.5 0.1 convert_reduce_fusion.1
  175.7 6.7 %collective-permute-start.7 = (bf16[192,256]{1,0:T(8,128)(2,1)S(1)}, bf16[192,256]{1,0:T(8,128)(2,1)S(1)}, u32[]{:S(2)}, u32[]{:S(2)}) collective-permute-start(bf16[192,256]{1,0:T(8,128)(2,1)S(1)} %fusion.11), channel_id=1, source_target_pairs={{0,496},{16,0},{32,16},{48,32},{64,48},{80,64},{96,80},{112,96},{1... | collective-permute-start | bytes 294920 | tf_op jit(solution)/shard_map/ppermute | solution.py:276
  182.4 1.9 collective-permute-start.8
  184.3 0.3 fusion.1
  184.6 0.0 collective-permute-done.7
  184.6 0.3 convolution_add_fusion.1
  185.0 6.4 %collective-permute-done.8 = bf16[192,256]{1,0:T(8,128)(2,1)S(1)} collective-permute-done((bf16[192,256]{1,0:T(8,128)(2,1)S(1)}, bf16[192,256]{1,0:T(8,128)(2,1)S(1)}, u32[]{:S(2)}, u32[]{:S(2)}) %collective-permute-start.8) | collective-permute-done | bytes 98336 | tf_op jit(solution)/shard_map/ppermute | solution.py:276
  191.4 0.3 fusion
  191.7 0.8 copy.14
  (12 shorter events, 0.1 us)
Async XLA Ops:
  6.5 21.1 %collective-permute-start = (bf16[256,192]{1,0:T(8,128)(2,1)}, bf16[256,192]{1,0:T(8,128)(2,1)S(1)}, u32[]{:S(2)}, u32[]{:S(2)}) collective-permute-start(bf16[256,192]{1,0:T(8,128)(2,1)} %bitcast.63), channel_id=1, source_target_pairs={{0,16},{16,32},{32,48},{48,64},{64,80},{80,96},{96,112},{112,128},... | collective-permute-start | bytes 294920 | tf_op jit(solution)/shard_map/ppermute | solution.py:276
  12.0 15.7 %collective-permute-start.1 = (bf16[256,192]{1,0:T(8,128)(2,1)}, bf16[256,192]{1,0:T(8,128)(2,1)S(1)}, u32[]{:S(2)}, u32[]{:S(2)}) collective-permute-start(bf16[256,192]{1,0:T(8,128)(2,1)} %bitcast.64), channel_id=1, source_target_pairs={{0,496},{16,0},{32,16},{48,32},{64,48},{80,64},{96,80},{112,96},{1... | collective-permute-start | bytes 294920 | tf_op jit(solution)/shard_map/ppermute | solution.py:276
  25.7 7.4 %collective-permute-start.2 = (bf16[96,512]{1,0:T(8,128)(2,1)S(1)}, bf16[96,512]{1,0:T(8,128)(2,1)S(1)}, u32[]{:S(2)}, u32[]{:S(2)}) collective-permute-start(bf16[96,512]{1,0:T(8,128)(2,1)S(1)} %pad_maximum_fusion), channel_id=1, source_target_pairs={{0,0},{1,16},{16,1},{17,17},{2,2},{3,18},{18,3},{19,19},{4,4},{5,2... | collective-permute-start | bytes 294920 | tf_op jit(solution)/shard_map/ppermute | solution.py:301
  27.7 0.7 copy-start.2
  28.4 0.9 copy-start.4
  30.4 1.4 copy-start.1
  33.2 40.5 %all-to-all-start = ((bf16[32,288,128]{2,1,0:T(8,128)(2,1)}), bf16[32,288,128]{2,1,0:T(8,128)(2,1)S(1)}, u32[]{:S(2)}, u32[]{:S(2)}) async-start(bf16[32,288,128]{2,1,0:T(8,128)(2,1)} %copy-done.1), calls=%async_computation | async-start | bytes 4718592 | tf_op jit(solution)/shard_map/all_to_all | solution.py:338
  39.5 57.1 %copy-start.5 = (f32[2,2,128]{2,1,0:T(2,128)S(1)}, f32[2,2,128]{2,1,0:T(2,128)}, u32[]{:S(2)}) copy-start(f32[2,2,128]{2,1,0:T(2,128)} %param.10) | copy-start | bytes 6148
  39.5 59.0 %copy-start.3 = (s32[2,2]{1,0:T(2,128)S(1)}, s32[2,2]{1,0:T(2,128)}, u32[]{:S(2)}) copy-start(s32[2,2]{1,0:T(2,128)} %shifts.5) | copy-start | bytes 52
  39.5 111.0 %all-gather.2.cloned.1.call-start = ((), (), s32[]{:S(2)}) async-start(), calls=%async_computation.4 | async-start | bytes 6488064 | tf_op jit(solution)/shard_map/all_gather | solution.py:346
  40.4 33.2 %collective-permute-start.3 = (bf16[96,512]{1,0:T(8,128)(2,1)}, bf16[96,512]{1,0:T(8,128)(2,1)S(1)}, u32[]{:S(2)}, u32[]{:S(2)}) collective-permute-start(bf16[96,512]{1,0:T(8,128)(2,1)} %get-tuple-element.26), channel_id=1, source_target_pairs={{0,16},{16,0},{1,17},{17,1},{2,18},{18,2},{3,19},{19,3},{4,20},{20... | collective-permute-start | bytes 294920 | tf_op jit(solution)/shard_map/ppermute | solution.py:305
  74.4 13.6 %collective-permute-start.4 = (bf16[768,512]{1,0:T(8,128)(2,1)S(1)}, bf16[768,512]{1,0:T(8,128)(2,1)S(1)}, u32[]{:S(2)}, u32[]{:S(2)}) collective-permute-start(bf16[768,512]{1,0:T(8,128)(2,1)S(1)} %all_gather.7.refs_0_), channel_id=1, source_target_pairs={{0,32},{1,481},{32,64},{33,1},{64,96},{65,33},{96,128},{97,65},{12... | collective-permute-start | bytes 2359304 | tf_op jit(solution)/shard_map/ppermute | solution.py:348
  77.7 19.5 %collective-permute-start.5 = (bf16[768,512]{1,0:T(8,128)(2,1)S(1)}, bf16[768,512]{1,0:T(8,128)(2,1)S(1)}, u32[]{:S(2)}, u32[]{:S(2)}) collective-permute-start(bf16[768,512]{1,0:T(8,128)(2,1)S(1)} %all_gather.7.refs_0_), channel_id=1, source_target_pairs={{0,1},{1,0},{2,3},{3,2},{4,5},{5,4},{6,7},{7,6},{8,9},{9,8},{10,11... | collective-permute-start | bytes 2359304 | tf_op jit(solution)/shard_map/ppermute | solution.py:280
  88.0 10.6 %collective-permute-start.6 = (bf16[768,512]{1,0:T(8,128)(2,1)S(1)}, bf16[768,512]{1,0:T(8,128)(2,1)S(1)}, u32[]{:S(2)}, u32[]{:S(2)}) collective-permute-start(bf16[768,512]{1,0:T(8,128)(2,1)S(1)} %collective-permute-done.4.refs_1_), channel_id=1, source_target_pairs={{0,1},{1,0},{2,3},{3,2},{4,5},{5,4},{6,7},{7,6},{8,9},{9,8},{10,11... | collective-permute-start | bytes 2359304 | tf_op jit(solution)/shard_map/ppermute | solution.py:280
  101.9 1.1 copy-start
  103.1 27.6 %all-to-all-start.1 = ((bf16[32,192,128]{2,1,0:T(8,128)(2,1)}), bf16[32,192,128]{2,1,0:T(8,128)(2,1)S(1)}, u32[]{:S(2)}, u32[]{:S(2)}) async-start(bf16[32,192,128]{2,1,0:T(8,128)(2,1)} %bitcast.62), calls=%async_computation.1 | async-start | bytes 3145728 | tf_op jit(solution)/shard_map/all_to_all | solution.py:358
  157.2 18.3 %all-to-all-start.3 = ((bf16[16,192,128]{2,1,0:T(8,128)(2,1)}), bf16[16,192,128]{2,1,0:T(8,128)(2,1)S(1)}, u32[]{:S(2)}, u32[]{:S(2)}) async-start(bf16[16,192,128]{2,1,0:T(8,128)(2,1)} %bitcast.68), calls=%async_computation.3 | async-start | bytes 1572864 | tf_op jit(solution)/shard_map/all_to_all | solution.py:375
  175.7 9.0 %collective-permute-start.7 = (bf16[192,256]{1,0:T(8,128)(2,1)S(1)}, bf16[192,256]{1,0:T(8,128)(2,1)S(1)}, u32[]{:S(2)}, u32[]{:S(2)}) collective-permute-start(bf16[192,256]{1,0:T(8,128)(2,1)S(1)} %fusion.11), channel_id=1, source_target_pairs={{0,496},{16,0},{32,16},{48,32},{64,48},{80,64},{96,80},{112,96},{1... | collective-permute-start | bytes 294920 | tf_op jit(solution)/shard_map/ppermute | solution.py:276
  182.4 9.0 %collective-permute-start.8 = (bf16[192,256]{1,0:T(8,128)(2,1)S(1)}, bf16[192,256]{1,0:T(8,128)(2,1)S(1)}, u32[]{:S(2)}, u32[]{:S(2)}) collective-permute-start(bf16[192,256]{1,0:T(8,128)(2,1)S(1)} %fusion.11), channel_id=1, source_target_pairs={{0,16},{16,32},{32,48},{48,64},{64,80},{80,96},{96,112},{112,128},... | collective-permute-start | bytes 294920 | tf_op jit(solution)/shard_map/ppermute | solution.py:276
Sparse Core Ops, SparseCore 0:
  74.5 75.9 all-gather.1

commit v5 on v4

--- a/solution.py
+++ b/solution.py
@@ -11,7 +11,7 @@
 WH = 4
 WW = 8
 UNITS = 4
-CHUNKS = 8
+CHUNKS = 4
 TP = ("xl", "y", "c")
 SP = ("z8", "z2", "xh")
 NT = (((1,), (1,)), ((), ()))
@@ -39,8 +39,11 @@
 def block_kernel(spec, weights_are_pairs, shifts, x_ref, qk_gain_ref, *refs):
     copies = []
     if weights_are_pairs:
-        source, out_ref, x_rows_ref, held_ref, sems = refs
+        source, out_hbm, x_rows_ref, held_ref, x_held, out_ref, sems = refs
         weights = [held_ref]
+        fetch = pltpu.make_async_copy(x_ref, x_held, sems.at[CHUNKS])
+        fetch.start()
+        x_ref = x_held
         size = source.shape[0] // CHUNKS
         for n in range(CHUNKS):
             there = slice(n * size, (n + 1) * size)
@@ -80,6 +83,9 @@
         row_window = lax.shift_right_logical(row + shift_row, WH.bit_length() - 1)
         return row_window * 16 + lax.shift_right_logical(col, WW.bit_length() - 1)
 
+    if copies:
+        fetch.wait()
+    sent = []
     scales = []
     for w in range(windows):
         squares = jnp.zeros((rows, tokens), jnp.float32)
@@ -143,6 +149,16 @@
                 out_ref[slab, order[u + k]] = total[
                     k * rows : (k + 1) * rows, slab * tokens : (slab + 1) * tokens
                 ]
+        if copies:
+            made = (slice(0, slabs), slice(u, u + UNITS))
+            sent.append(
+                pltpu.make_async_copy(
+                    out_ref.at[made], out_hbm.at[made], sems.at[CHUNKS + 1 + u // UNITS]
+                )
+            )
+            sent[-1].start()
+    for copy in sent:
+        copy.wait()
 
 
 class Spec:
@@ -197,16 +213,18 @@
     if len(weights) == 1:
         scratch += [
             pltpu.VMEM(weights[0].shape, jnp.bfloat16),
-            pltpu.SemaphoreType.DMA((CHUNKS,)),
+            pltpu.VMEM(x.shape, jnp.bfloat16),
+            pltpu.VMEM((spec.slabs, units, rows, tokens), jnp.bfloat16),
+            pltpu.SemaphoreType.DMA((CHUNKS + 1 + units // UNITS,)),
         ]
     vmem = pl.BlockSpec(memory_space=pltpu.VMEM)
     smem = pl.BlockSpec(memory_space=pltpu.SMEM)
+    place = pl.BlockSpec(memory_space=pl.ANY) if len(weights) == 1 else vmem
     return pl.pallas_call(
         functools.partial(block_kernel, spec, len(weights) == 1),
         out_shape=jax.ShapeDtypeStruct((spec.slabs, units, rows, tokens), jnp.bfloat16),
-        in_specs=[smem, vmem, vmem]
-        + [pl.BlockSpec(memory_space=pl.ANY) if len(weights) == 1 else vmem] * len(weights),
-        out_specs=vmem,
+        in_specs=[smem, place, vmem] + [place] * len(weights),
+        out_specs=place,
         scratch_shapes=scratch,
         compiler_params=pltpu.CompilerParams(
             vmem_limit_bytes=(58 if len(weights) == 1 else 40) * 1024 * 1024

time: 200 us -> 199 us (level)
  no operation moved by 1% of the time
where the time goes in v5:
time: 199 us; the launch traced here: 198 us
  starting transfers between devices  65.7 us (33%)
  waiting for transfers between devices  47.4 us (24%)
  blocking collectives  45.1 us (23%)
  between operations  15.8 us (8%)
  Pallas kernels  10.4 us (5%)
  local copies, waits for them, and re-layouts  8.18 us (4%)
  other arithmetic  4.72 us (2%)
    all_gather x1, blocking collectives, on_device(): near0 = lax.all_gather(turned, 'z8', axis=0, tiled=True)  28.4 us
    ppermute x4, starting transfers between devices, neighbour(): lax.ppermute(x, SP, [(i, (i - distance) % count) for i in range(count)])  25 us
    all_to_all x1, waiting for transfers between devices, on_device(): lax.all_to_all(sums.reshape(2 * tp_count, local, half), ('xh',) + TP, 0,...  20.8 us
    all_to_all x1, blocking collectives, on_device(): lax.all_to_all(spread([x_t[:, :half], x_t[:, half:]], tp_count // 2), TP,...  16.6 us
    ppermute x2, starting transfers between devices, swap_cores(): return lax.ppermute(x, 'c', [(0, 1), (1, 0)])  14.2 us
    all_to_all x1, waiting for transfers between devices, on_device(): lax.all_to_all(sums.reshape(tp_count, local, half), TP, 0, 0, tiled=True)  10.3 us
    pallas_call x2, Pallas kernels, run_block(): pl.pallas_call(functools.partial(block_kernel, spec, len(weights) == 1),...  9.3 us
    ppermute x4, waiting for transfers between devices, neighbour(): lax.ppermute(x, SP, [(i, (i - distance) % count) for i in range(count)])  6.4 us
  transfers between devices with their start and end apart: 13, of which 7 were waited for; matrix products, arithmetic and copies ran while one was open for 4% of the time, Pallas kernels for 2%

profile of v5, /device:TPU:1, one launch (start us, length us, event | category | flops | bytes accessed | tf_op | source)
XLA Modules:
  0.0 198.5 jit_solution(6319149703892669565)
XLA Ops:
  6.5 5.5 %collective-permute-start = (bf16[256,192]{1,0:T(8,128)(2,1)}, bf16[256,192]{1,0:T(8,128)(2,1)S(1)}, u32[]{:S(2)}, u32[]{:S(2)}) collective-permute-start(bf16[256,192]{1,0:T(8,128)(2,1)} %bitcast.63), channel_id=1, source_target_pairs={{0,16},{16,32},{32,48},{48,64},{64,80},{80,96},{96,112},{112,128},... | collective-permute-start | bytes 294920 | tf_op jit(solution)/shard_map/ppermute | solution.py:294
  12.0 10.9 %collective-permute-start.1 = (bf16[256,192]{1,0:T(8,128)(2,1)}, bf16[256,192]{1,0:T(8,128)(2,1)S(1)}, u32[]{:S(2)}, u32[]{:S(2)}) collective-permute-start(bf16[256,192]{1,0:T(8,128)(2,1)} %bitcast.64), channel_id=1, source_target_pairs={{0,496},{16,0},{32,16},{48,32},{64,48},{80,64},{96,80},{112,96},{1... | collective-permute-start | bytes 294920 | tf_op jit(solution)/shard_map/ppermute | solution.py:294
  22.9 0.8 fusion.52
  23.7 0.9 slice_convert_fusion
  24.7 0.1 copy.12
  24.8 0.8 slice_bitcast_fusion.6
  25.6 0.1 dynamic-slice_bitcast_fusion
  25.6 0.1 fusion.13
  25.7 1.9 collective-permute-start.2
  27.7 0.0 collective-permute-done.before_ref
  27.7 0.0 collective-permute-done.1.after_ref
  27.7 0.0 copy-start.2
  27.7 0.7 copy-done.2
  28.4 0.9 copy-done.4
  29.3 1.1 arrange_tokens.1
  30.4 0.0 copy-start.1
  30.4 1.4 copy-done.1
  31.8 1.4 collective-permute-done.2
  33.2 6.3 %all-to-all-start = ((bf16[32,288,128]{2,1,0:T(8,128)(2,1)}), bf16[32,288,128]{2,1,0:T(8,128)(2,1)S(1)}, u32[]{:S(2)}, u32[]{:S(2)}) async-start(bf16[32,288,128]{2,1,0:T(8,128)(2,1)} %copy-done.1), calls=%async_computation | async-start | bytes 4718592 | tf_op jit(solution)/shard_map/all_to_all | solution.py:356
  39.5 0.0 copy-start.5
  39.5 0.0 copy-start.3
  39.5 0.0 all-gather.2.cloned.1.call-start
  39.6 0.1 copy.13
  39.7 0.1 fusion.12
  39.8 0.7 fusion.51
  40.4 4.8 %collective-permute-start.3 = (bf16[96,512]{1,0:T(8,128)(2,1)}, bf16[96,512]{1,0:T(8,128)(2,1)S(1)}, u32[]{:S(2)}, u32[]{:S(2)}) collective-permute-start(bf16[96,512]{1,0:T(8,128)(2,1)} %get-tuple-element.26), channel_id=1, source_target_pairs={{0,16},{16,0},{1,17},{17,1},{2,18},{18,2},{3,19},{19,3},{4,20},{20... | collective-permute-start | bytes 294920 | tf_op jit(solution)/shard_map/ppermute | solution.py:323
  45.2 28.4 %all_gather.7.refs_0_ = bf16[768,512]{1,0:T(8,128)(2,1)S(1)} all-gather(bf16[96,512]{1,0:T(8,128)(2,1)S(1)} %collective-permute-done.2), channel_id=1, replica_groups=mesh['z8'=8,'z2'=2,'xh'=2,'xl'=2,'y'=4,'c'=2] {'z8'}, dimensions={0}, use_global_device_ids=true | all-gather | bytes 884736 | tf_op jit(solution)/shard_map/all_gather | solution.py:357
  73.6 0.0 collective-permute-done.3
  73.6 0.0 all-to-all-done
  73.7 0.7 maximum_select_fusion
  74.4 0.0 all-gather.2.cloned.1.call-update
  74.4 3.3 %collective-permute-start.4 = (bf16[768,512]{1,0:T(8,128)(2,1)S(1)}, bf16[768,512]{1,0:T(8,128)(2,1)S(1)}, u32[]{:S(2)}, u32[]{:S(2)}) collective-permute-start(bf16[768,512]{1,0:T(8,128)(2,1)S(1)} %all_gather.7.refs_0_), channel_id=1, source_target_pairs={{0,32},{1,481},{32,64},{33,1},{64,96},{65,33},{96,128},{97,65},{12... | collective-permute-start | bytes 2359304 | tf_op jit(solution)/shard_map/ppermute | solution.py:366
  77.7 5.7 %collective-permute-start.5 = (bf16[768,512]{1,0:T(8,128)(2,1)S(1)}, bf16[768,512]{1,0:T(8,128)(2,1)S(1)}, u32[]{:S(2)}, u32[]{:S(2)}) collective-permute-start(bf16[768,512]{1,0:T(8,128)(2,1)S(1)} %all_gather.7.refs_0_), channel_id=1, source_target_pairs={{0,1},{1,0},{2,3},{3,2},{4,5},{5,4},{6,7},{7,6},{8,9},{9,8},{10,11... | collective-permute-start | bytes 2359304 | tf_op jit(solution)/shard_map/ppermute | solution.py:298
  83.3 4.6 %collective-permute-done.4.refs_1_ = bf16[768,512]{1,0:T(8,128)(2,1)S(1)} collective-permute-done((bf16[768,512]{1,0:T(8,128)(2,1)S(1)}, bf16[768,512]{1,0:T(8,128)(2,1)S(1)}, u32[]{:S(2)}, u32[]{:S(2)}) %collective-permute-start.4) | collective-permute-done | bytes 786464 | tf_op jit(solution)/shard_map/ppermute | solution.py:366
  88.0 8.6 %collective-permute-start.6 = (bf16[768,512]{1,0:T(8,128)(2,1)S(1)}, bf16[768,512]{1,0:T(8,128)(2,1)S(1)}, u32[]{:S(2)}, u32[]{:S(2)}) collective-permute-start(bf16[768,512]{1,0:T(8,128)(2,1)S(1)} %collective-permute-done.4.refs_1_), channel_id=1, source_target_pairs={{0,1},{1,0},{2,3},{3,2},{4,5},{5,4},{6,7},{7,6},{8,9},{9,8},{10,11... | collective-permute-start | bytes 2359304 | tf_op jit(solution)/shard_map/ppermute | solution.py:298
  96.6 0.0 copy-done.5
  96.6 0.6 slice_bitcast_fusion.8
  97.1 0.0 collective-permute-done.5.refs_2_
  97.2 1.4 collective-permute-done.6.refs_3_
  98.5 0.0 copy-done.3
  98.5 3.4 %window_block.2 = bf16[2,32,96,128]{3,2,1,0:T(8,128)(2,1)S(1)} custom-call(s32[2,2]{1,0:T(2,128)S(1)} %copy-done.3, bf16[96,96,128]{2,1,0:T(8,128)(2,1)S(1)} %bitcast.61, f32[2,128]{1,0:T(2,128)S(1)} %get-tuple-element.34.qk_gain_ref, bf16[768,512]{1,0:T(8,128)(2,1)S(1)} %all_gather.7.refs_0_, bf16[768,512]{1,0:T(8,128)(2,1)S(1)} %collective-permute-done.4.refs_1_, ...), custom_call_target="tpu_custom_call" | custom-call | flops 1207959552 | bytes 7864320 | tf_op jit(solution)/shard_map/window_block/pallas_call | solution.py:223
  101.9 1.1 copy-done
  103.1 4.9 %all-to-all-start.1 = ((bf16[32,192,128]{2,1,0:T(8,128)(2,1)}), bf16[32,192,128]{2,1,0:T(8,128)(2,1)S(1)}, u32[]{:S(2)}, u32[]{:S(2)}) async-start(bf16[32,192,128]{2,1,0:T(8,128)(2,1)} %bitcast.62), calls=%async_computation.1 | async-start | bytes 3145728 | tf_op jit(solution)/shard_map/all_to_all | solution.py:376
  108.0 0.6 fusion.53
  108.7 1.2 and_select_fusion
  109.9 20.8 %all-to-all-done.1 = bf16[32,192,128]{2,1,0:T(8,128)(2,1)S(1)} async-done(((bf16[32,192,128]{2,1,0:T(8,128)(2,1)}), bf16[32,192,128]{2,1,0:T(8,128)(2,1)S(1)}, u32[]{:S(2)}, u32[]{:S(2)}) %all-to-all-start.1) | async-done | bytes 1572896 | tf_op jit(solution)/shard_map/all_to_all | solution.py:376
  130.7 0.2 convert_reduce_fusion
  130.9 0.3 convolution_convert_fusion
  131.3 0.1 broadcast_in_dim.2
  131.4 16.6 %all_to_all.20 = bf16[16,192,128]{2,1,0:T(8,128)(2,1)} all-to-all(bf16[16,192,128]{2,1,0:T(8,128)(2,1)S(1)} %bitcast.70), channel_id=1, replica_groups=mesh['z8'=8,'z2'=2,'xh'=2,'xl'=2,'y'=4,'c'=2] {'xl','y','c'}, dimensions={0} | all-to-all | bytes 1572864 | tf_op jit(solution)/shard_map/all_to_all | solution.py:385
  148.1 2.4 %all-gather.2.cloned.1.call-done = bf16[32,192,512]{2,1,0:T(8,128)(2,1)} async-done(((bf16[1,192,512]{2,1,0:T(8,128)(2,1)}), bf16[32,192,512]{2,1,0:T(8,128)(2,1)}) %all-gather.2.cloned.1.call-update) | async-done | bytes 6291472 | tf_op jit(solution)/shard_map/all_gather | solution.py:364
  150.5 5.9 %window_block.3 = bf16[1,32,96,128]{3,2,1,0:T(8,128)(2,1)} custom-call(s32[2,2]{1,0:T(2,128)} %shifts.5, bf16[32,96,128]{2,1,0:T(8,128)(2,1)} %bitcast.69, f32[2,128]{1,0:T(2,128)} %get-tuple-element.33.qk_gain_ref, bf16[16,2,192,512]{3,2,1,0:T(8,128)(2,1)} %bitcast.67), custom_call_target="tpu_custom_call" | custom-call | flops 805306368 | bytes 7864320 | tf_op jit(solution)/shard_map/window_block/pallas_call | solution.py:223
  156.4 5.3 %all-to-all-start.3 = ((bf16[16,192,128]{2,1,0:T(8,128)(2,1)}), bf16[16,192,128]{2,1,0:T(8,128)(2,1)S(1)}, u32[]{:S(2)}, u32[]{:S(2)}) async-start(bf16[16,192,128]{2,1,0:T(8,128)(2,1)} %bitcast.68), calls=%async_computation.3 | async-start | bytes 1572864 | tf_op jit(solution)/shard_map/all_to_all | solution.py:393
  163.8 0.6 and_select_fusion.2
  164.4 10.3 %all-to-all-done.3 = bf16[16,192,128]{2,1,0:T(8,128)(2,1)S(1)} async-done(((bf16[16,192,128]{2,1,0:T(8,128)(2,1)}), bf16[16,192,128]{2,1,0:T(8,128)(2,1)S(1)}, u32[]{:S(2)}, u32[]{:S(2)}) %all-to-all-start.3) | async-done | bytes 786464 | tf_op jit(solution)/shard_map/all_to_all | solution.py:393
  174.7 0.1 convert_reduce_fusion.1
  174.9 6.7 %collective-permute-start.7 = (bf16[192,256]{1,0:T(8,128)(2,1)S(1)}, bf16[192,256]{1,0:T(8,128)(2,1)S(1)}, u32[]{:S(2)}, u32[]{:S(2)}) collective-permute-start(bf16[192,256]{1,0:T(8,128)(2,1)S(1)} %fusion.11), channel_id=1, source_target_pairs={{0,496},{16,0},{32,16},{48,32},{64,48},{80,64},{96,80},{112,96},{1... | collective-permute-start | bytes 294920 | tf_op jit(solution)/shard_map/ppermute | solution.py:294
  181.6 1.9 collective-permute-start.8
  183.5 0.3 fusion.1
  183.8 0.0 collective-permute-done.7
  183.8 0.3 convolution_add_fusion.1
  184.2 6.4 %collective-permute-done.8 = bf16[192,256]{1,0:T(8,128)(2,1)S(1)} collective-permute-done((bf16[192,256]{1,0:T(8,128)(2,1)S(1)}, bf16[192,256]{1,0:T(8,128)(2,1)S(1)}, u32[]{:S(2)}, u32[]{:S(2)}) %collective-permute-start.8) | collective-permute-done | bytes 98336 | tf_op jit(solution)/shard_map/ppermute | solution.py:294
  190.6 0.3 fusion
  190.9 0.8 copy.14
  (12 shorter events, 0.1 us)
Async XLA Ops:
  6.5 21.1 %collective-permute-start = (bf16[256,192]{1,0:T(8,128)(2,1)}, bf16[256,192]{1,0:T(8,128)(2,1)S(1)}, u32[]{:S(2)}, u32[]{:S(2)}) collective-permute-start(bf16[256,192]{1,0:T(8,128)(2,1)} %bitcast.63), channel_id=1, source_target_pairs={{0,16},{16,32},{32,48},{48,64},{64,80},{80,96},{96,112},{112,128},... | collective-permute-start | bytes 294920 | tf_op jit(solution)/shard_map/ppermute | solution.py:294
  12.0 15.7 %collective-permute-start.1 = (bf16[256,192]{1,0:T(8,128)(2,1)}, bf16[256,192]{1,0:T(8,128)(2,1)S(1)}, u32[]{:S(2)}, u32[]{:S(2)}) collective-permute-start(bf16[256,192]{1,0:T(8,128)(2,1)} %bitcast.64), channel_id=1, source_target_pairs={{0,496},{16,0},{32,16},{48,32},{64,48},{80,64},{96,80},{112,96},{1... | collective-permute-start | bytes 294920 | tf_op jit(solution)/shard_map/ppermute | solution.py:294
  25.7 7.4 %collective-permute-start.2 = (bf16[96,512]{1,0:T(8,128)(2,1)S(1)}, bf16[96,512]{1,0:T(8,128)(2,1)S(1)}, u32[]{:S(2)}, u32[]{:S(2)}) collective-permute-start(bf16[96,512]{1,0:T(8,128)(2,1)S(1)} %pad_maximum_fusion), channel_id=1, source_target_pairs={{0,0},{1,16},{16,1},{17,17},{2,2},{3,18},{18,3},{19,19},{4,4},{5,2... | collective-permute-start | bytes 294920 | tf_op jit(solution)/shard_map/ppermute | solution.py:319
  27.7 0.7 copy-start.2
  28.4 0.9 copy-start.4
  30.4 1.4 copy-start.1
  33.2 40.5 %all-to-all-start = ((bf16[32,288,128]{2,1,0:T(8,128)(2,1)}), bf16[32,288,128]{2,1,0:T(8,128)(2,1)S(1)}, u32[]{:S(2)}, u32[]{:S(2)}) async-start(bf16[32,288,128]{2,1,0:T(8,128)(2,1)} %copy-done.1), calls=%async_computation | async-start | bytes 4718592 | tf_op jit(solution)/shard_map/all_to_all | solution.py:356
  39.5 57.1 %copy-start.5 = (f32[2,2,128]{2,1,0:T(2,128)S(1)}, f32[2,2,128]{2,1,0:T(2,128)}, u32[]{:S(2)}) copy-start(f32[2,2,128]{2,1,0:T(2,128)} %param.10) | copy-start | bytes 6148
  39.5 59.0 %copy-start.3 = (s32[2,2]{1,0:T(2,128)S(1)}, s32[2,2]{1,0:T(2,128)}, u32[]{:S(2)}) copy-start(s32[2,2]{1,0:T(2,128)} %shifts.5) | copy-start | bytes 52
  39.5 111.0 %all-gather.2.cloned.1.call-start = ((), (), s32[]{:S(2)}) async-start(), calls=%async_computation.4 | async-start | bytes 6488064 | tf_op jit(solution)/shard_map/all_gather | solution.py:364
  40.4 33.2 %collective-permute-start.3 = (bf16[96,512]{1,0:T(8,128)(2,1)}, bf16[96,512]{1,0:T(8,128)(2,1)S(1)}, u32[]{:S(2)}, u32[]{:S(2)}) collective-permute-start(bf16[96,512]{1,0:T(8,128)(2,1)} %get-tuple-element.26), channel_id=1, source_target_pairs={{0,16},{16,0},{1,17},{17,1},{2,18},{18,2},{3,19},{19,3},{4,20},{20... | collective-permute-start | bytes 294920 | tf_op jit(solution)/shard_map/ppermute | solution.py:323
  74.4 13.6 %collective-permute-start.4 = (bf16[768,512]{1,0:T(8,128)(2,1)S(1)}, bf16[768,512]{1,0:T(8,128)(2,1)S(1)}, u32[]{:S(2)}, u32[]{:S(2)}) collective-permute-start(bf16[768,512]{1,0:T(8,128)(2,1)S(1)} %all_gather.7.refs_0_), channel_id=1, source_target_pairs={{0,32},{1,481},{32,64},{33,1},{64,96},{65,33},{96,128},{97,65},{12... | collective-permute-start | bytes 2359304 | tf_op jit(solution)/shard_map/ppermute | solution.py:366
  77.7 19.5 %collective-permute-start.5 = (bf16[768,512]{1,0:T(8,128)(2,1)S(1)}, bf16[768,512]{1,0:T(8,128)(2,1)S(1)}, u32[]{:S(2)}, u32[]{:S(2)}) collective-permute-start(bf16[768,512]{1,0:T(8,128)(2,1)S(1)} %all_gather.7.refs_0_), channel_id=1, source_target_pairs={{0,1},{1,0},{2,3},{3,2},{4,5},{5,4},{6,7},{7,6},{8,9},{9,8},{10,11... | collective-permute-start | bytes 2359304 | tf_op jit(solution)/shard_map/ppermute | solution.py:298
  88.0 10.6 %collective-permute-start.6 = (bf16[768,512]{1,0:T(8,128)(2,1)S(1)}, bf16[768,512]{1,0:T(8,128)(2,1)S(1)}, u32[]{:S(2)}, u32[]{:S(2)}) collective-permute-start(bf16[768,512]{1,0:T(8,128)(2,1)S(1)} %collective-permute-done.4.refs_1_), channel_id=1, source_target_pairs={{0,1},{1,0},{2,3},{3,2},{4,5},{5,4},{6,7},{7,6},{8,9},{9,8},{10,11... | collective-permute-start | bytes 2359304 | tf_op jit(solution)/shard_map/ppermute | solution.py:298
  101.9 1.1 copy-start
  103.1 27.6 %all-to-all-start.1 = ((bf16[32,192,128]{2,1,0:T(8,128)(2,1)}), bf16[32,192,128]{2,1,0:T(8,128)(2,1)S(1)}, u32[]{:S(2)}, u32[]{:S(2)}) async-start(bf16[32,192,128]{2,1,0:T(8,128)(2,1)} %bitcast.62), calls=%async_computation.1 | async-start | bytes 3145728 | tf_op jit(solution)/shard_map/all_to_all | solution.py:376
  156.4 18.3 %all-to-all-start.3 = ((bf16[16,192,128]{2,1,0:T(8,128)(2,1)}), bf16[16,192,128]{2,1,0:T(8,128)(2,1)S(1)}, u32[]{:S(2)}, u32[]{:S(2)}) async-start(bf16[16,192,128]{2,1,0:T(8,128)(2,1)} %bitcast.68), calls=%async_computation.3 | async-start | bytes 1572864 | tf_op jit(solution)/shard_map/all_to_all | solution.py:393
  174.9 9.0 %collective-permute-start.7 = (bf16[192,256]{1,0:T(8,128)(2,1)S(1)}, bf16[192,256]{1,0:T(8,128)(2,1)S(1)}, u32[]{:S(2)}, u32[]{:S(2)}) collective-permute-start(bf16[192,256]{1,0:T(8,128)(2,1)S(1)} %fusion.11), channel_id=1, source_target_pairs={{0,496},{16,0},{32,16},{48,32},{64,48},{80,64},{96,80},{112,96},{1... | collective-permute-start | bytes 294920 | tf_op jit(solution)/shard_map/ppermute | solution.py:294
  181.6 9.0 %collective-permute-start.8 = (bf16[192,256]{1,0:T(8,128)(2,1)S(1)}, bf16[192,256]{1,0:T(8,128)(2,1)S(1)}, u32[]{:S(2)}, u32[]{:S(2)}) collective-permute-start(bf16[192,256]{1,0:T(8,128)(2,1)S(1)} %fusion.11), channel_id=1, source_target_pairs={{0,16},{16,32},{32,48},{48,64},{64,80},{80,96},{96,112},{112,128},... | collective-permute-start | bytes 294920 | tf_op jit(solution)/shard_map/ppermute | solution.py:294
Sparse Core Ops, SparseCore 0:
  74.5 75.9 all-gather.1
